TPU v7x, 32 devices: a whole 2x2x4 slice. The times are simulated.
32 devices in a mesh: scene: 2 (over x), row: 16 (over z, y, core).
Axes of the slice: x: 2, y: 2, z: 4, core: 2. Of those that a mesh axis runs over, the one named last changes fastest.
Arguments:
- echoes: bfloat16 [2048, 2, 8192], P(('scene', 'row')), parts along dimension 0, may hold values from -6 to 6
- range_replica: bfloat16 [2, 1024], replicated, may hold values from -0.125 to 0.125
- azimuth_replicas: bfloat16 [16, 2, 512], replicated, may hold values from -0.1875 to 0.1875
- replica_index: int32 [16384], P(('scene', 'row')), parts along dimension 0, may hold values from 0 to 15
- azimuth_extent: int32 [128], P('scene'), parts along dimension 0, may hold values from 0 to 16
- range_extent: int32 [1024], P('scene'), parts along dimension 0, may hold values from 0 to 16
Outputs:
- focused: bfloat16 [2048, 2, 8192], P('scene', None, 'row'), parts along dimension 0
- looked: float32 [1024, 64], P(('scene', 'row')), parts along dimension 0
There are 2 independent parts, one for each index of `scene`. A program takes and returns all parts, laid end to end along the dimension named above; an argument that names none is the same for every part. Nothing has to cross between parts.
All inputs are finite; a program needn't handle non-finite values.
Results may differ from a plain program's by a relative error of at most 0.0049.
Values may be sent and summed in bfloat16 or wider, within the bound.
A program may use at most 128 MiB of HBM per device.

v0:
```python
import functools

import jax
import jax.numpy as jnp
import numpy as np
from jax import lax
from jax.experimental import pallas as pl
from jax.experimental.pallas import tpu as pltpu
from jax.sharding import PartitionSpec as P

TILE = 16
EXT = 16
CHUNKS = 2
HIGHEST = lax.Precision.HIGHEST
BF = jnp.bfloat16
F32 = jnp.float32


def mxu(left, right):
    return jnp.dot(left, right, preferred_element_type=F32)


def toeplitz_kernel(width, taps_ref, out_ref):
    for part in range(2):
        taps = jnp.broadcast_to(taps_ref[part : part + 1, :], (width, taps_ref.shape[1]))
        band = pltpu.roll(taps, 0, 1, stride=1, stride_axis=0)
        out_ref[:, part * width : (part + 1) * width] = band.T.astype(BF)


def toeplitz(range_replica, width):
    depth = range_replica.shape[1] + width
    taps = jnp.pad(range_replica.astype(F32), ((0, 0), (0, width)))
    return pl.pallas_call(
        functools.partial(toeplitz_kernel, width),
        out_shape=jax.ShapeDtypeStruct((depth, 2 * width), BF),
        name="toeplitz",
    )(taps)


def compress_kernel(group, bins, start, width, x_ref, t_ref, out_ref):
    step = pl.program_id(0)
    depth = t_ref.shape[0]
    rows = x_ref.shape[0]
    half = rows // 2
    windows = []
    for i in range(group):
        offset = pl.multiple_of((step * group + i) * bins + start, 128)
        windows.append(x_ref[:, pl.ds(offset, depth)])
    result = mxu(jnp.concatenate(windows, axis=0), t_ref[...])
    result = result.reshape(group, rows, 2 * width)
    out_ref[:, :half, :] = (result[:, :half, :width] + result[:, half:, width:]).astype(BF)
    out_ref[:, half:, :] = (result[:, half:, :width] - result[:, :half, width:]).astype(BF)


def compress(x, bands, devices, bins, start, width):
    rows = x.shape[0]
    group = max(1, min(devices, 1024 // rows))
    depth = bands.shape[0]
    return pl.pallas_call(
        functools.partial(compress_kernel, group, bins, start, width),
        grid=(devices // group,),
        in_specs=[
            pl.BlockSpec(x.shape, lambda g: (0, 0)),
            pl.BlockSpec(bands.shape, lambda g: (0, 0)),
        ],
        out_specs=pl.BlockSpec((group, rows, width), lambda g: (g, 0, 0)),
        out_shape=jax.ShapeDtypeStruct((devices, rows, width), BF),
        compiler_params=pltpu.CompilerParams(vmem_limit_bytes=48 * 2**20),
        cost_estimate=pl.CostEstimate(
            flops=2 * devices * rows * depth * 2 * width,
            bytes_accessed=4 * devices * rows * width,
            transcendentals=0,
        ),
        name="compress",
    )(x, bands)


def spectra_kernel(c_ref, s_ref, g_ref, out_ref):
    taps = g_ref.shape[1]
    gr, gi = g_ref[0], g_ref[1]
    c, s = c_ref[:, :taps], s_ref[:, :taps]
    real = mxu(c, gr) + mxu(s, gi)
    imag = mxu(c, gi) - mxu(s, gr)
    for part, value in enumerate((real, imag)):
        high = value.astype(BF)
        low = (value - high.astype(F32)).astype(BF)
        out_ref[part] = jnp.concatenate([high, low], axis=1)


def azimuth_kernel(c_ref, s_ref, y_ref, g_ref, index_ref, mask_ref, out_ref, sums_ref):
    devices, rows, width = y_ref.shape
    half = rows // 2
    pulses = devices * half
    c, s = c_ref[...], s_ref[...]
    yr = y_ref[:, :half, :].reshape(pulses, width)
    yi = y_ref[:, half:, :].reshape(pulses, width)
    fr = mxu(c, yr) + mxu(s, yi)
    fi = mxu(c, yi) - mxu(s, yr)
    replicas = g_ref.shape[2] // 2
    which = lax.rem(lax.broadcasted_iota(jnp.int32, (2 * replicas, width), 0), replicas)
    pick = (which == index_ref[...]).astype(BF)
    gr = mxu(g_ref[0], pick)
    gi = mxu(g_ref[1], pick)
    scale = 1.0 / pulses
    zr = ((fr * gr + fi * gi) * scale).astype(BF)
    zi = ((fi * gr - fr * gi) * scale).astype(BF)
    ar = mxu(c, zr) - mxu(s, zi)
    ai = mxu(c, zi) + mxu(s, zr)
    out_ref[0] = ar.astype(BF)
    out_ref[1] = ai.astype(BF)
    power = ar * ar + ai * ai
    high = power.astype(BF)
    low = (power - high.astype(F32)).astype(BF)
    mask = mask_ref[...]
    sums_ref[...] = mxu(mask, high) + mxu(mask, low)


def azimuth(cos, sin, y, spectra, index, mask):
    pulses, width = cos.shape[0], y.shape[2]
    return pl.pallas_call(
        azimuth_kernel,
        out_shape=(
            jax.ShapeDtypeStruct((2, pulses, width), BF),
            jax.ShapeDtypeStruct((mask.shape[0], width), F32),
        ),
        compiler_params=pltpu.CompilerParams(vmem_limit_bytes=56 * 2**20),
        cost_estimate=pl.CostEstimate(
            flops=16 * pulses * pulses * width,
            bytes_accessed=4 * pulses * pulses + 8 * pulses * width,
            transcendentals=0,
        ),
        name="azimuth",
    )(cos, sin, y, spectra, index, mask)


def dft_tables(length):
    steps = np.arange(length, dtype=np.int64)
    angles = (np.outer(steps, steps) % length) * (2.0 * np.pi / length)
    return jnp.asarray(np.cos(angles), dtype=BF), jnp.asarray(np.sin(angles), dtype=BF)


def window_columns(positions, starts, stops):
    inside = (positions[:, None] >= starts[None, :]) & (positions[:, None] < stops[None, :])
    return inside.astype(F32)


def per_device(
    echoes, range_replica, azimuth_replicas, replica_index, azimuth_extent, range_extent
):
    devices = lax.axis_size("row")
    local_pulses, _, samples = echoes.shape
    taps = range_replica.shape[1]
    pulses = local_pulses * devices
    range_bins = samples // devices
    chunks = CHUNKS if range_bins % (128 * CHUNKS) == 0 else 1
    width = range_bins // chunks

    bands = toeplitz(range_replica, width)
    rows = echoes.transpose(1, 0, 2).reshape(2 * local_pulses, samples)
    rows = jnp.pad(rows, ((0, 0), (0, taps)))
    cos, sin = dft_tables(pulses)
    spectra = pl.pallas_call(
        spectra_kernel,
        out_shape=jax.ShapeDtypeStruct((2, pulses, 2 * azimuth_replicas.shape[0]), BF),
        compiler_params=pltpu.CompilerParams(vmem_limit_bytes=48 * 2**20),
        name="spectra",
    )(cos, sin, azimuth_replicas.transpose(1, 2, 0))

    tile_rows = pulses // TILE
    pulse_start = jnp.arange(tile_rows, dtype=jnp.int32) * TILE - azimuth_extent
    pulse_stop = pulse_start + TILE + 2 * azimuth_extent
    pulse_mask = window_columns(jnp.arange(pulses, dtype=jnp.int32), pulse_start, pulse_stop).T
    pulse_count = (jnp.minimum(pulse_stop, pulses) - jnp.maximum(pulse_start, 0)).astype(F32)
    pulse_mask = pulse_mask.astype(BF)

    images, sums = [], []
    for q in range(chunks):
        packed = compress(rows, bands, devices, range_bins, q * width, width)
        turned = lax.all_to_all(packed, "row", split_axis=0, concat_axis=0, tiled=True)
        index = replica_index[q * width : (q + 1) * width].reshape(1, width)
        image, row_sum = azimuth(cos, sin, turned, spectra, index, pulse_mask)
        images.append(image)
        sums.append(row_sum)
    focused = jnp.concatenate(images, axis=2).transpose(1, 0, 2)
    ends = devices - 1
    before = lax.ppermute(sums[-1][:, width - EXT :], "row", [(i, i + 1) for i in range(ends)])
    after = lax.ppermute(sums[0][:, :EXT], "row", [(i + 1, i) for i in range(ends)])
    row_sums = jnp.concatenate([before, *sums, after], axis=1)

    local_tiles = range_bins // TILE
    device = lax.axis_index("row")
    tile_ids = device * local_tiles + jnp.arange(local_tiles, dtype=jnp.int32)
    local_extent = lax.dynamic_slice_in_dim(range_extent, device * local_tiles, local_tiles)
    range_start = tile_ids * TILE - local_extent
    range_stop = range_start + TILE + 2 * local_extent
    range_count = (
        jnp.minimum(range_stop, samples) - jnp.maximum(range_start, 0)
    ).astype(F32)
    positions = device * range_bins - EXT + jnp.arange(range_bins + 2 * EXT, dtype=jnp.int32)
    range_mask = window_columns(positions, range_start, range_stop)
    window_sums = jnp.einsum(
        "ct,ic->ti", range_mask, row_sums, precision=HIGHEST, preferred_element_type=F32
    )
    looked = window_sums / (range_count[:, None] * pulse_count[None, :])
    return (focused, looked)


def solution(mesh):
    return jax.shard_map(
        per_device,
        mesh=mesh,
        in_specs=(
            P(("scene", "row"), None, None),
            P(),
            P(),
            P(("scene", "row")),
            P("scene"),
            P("scene"),
        ),
        out_specs=(P("scene", None, "row"), P(("scene", "row"), None)),
        check_vma=False,
    )
```

profile of v0, /device:TPU:15, one launch (start us, length us, event | category | flops | bytes accessed | tf_op | source)
XLA Modules:
  0.0 99.2 jit_solution(718788618708576934)
XLA Ops:
  0.6 1.3 %pad_convert_fusion.taps_ref = f32[2,1280]{1,0:T(2,128)} fusion(bf16[2,1024]{1,0:T(2,128)(2,1)} %param.9), kind=kLoop, calls=%fused_computation.17 | loop fusion | flops 2560 | bytes 14336 | tf_op jit(solution)/shard_map/jit(_pad)/pad | solution.py:32
  1.9 2.2 %toeplitz.1.t_ref = bf16[1280,512]{1,0:T(8,128)(2,1)} custom-call(f32[2,1280]{1,0:T(2,128)} %pad_convert_fusion.taps_ref), custom_call_target="tpu_custom_call" | custom-call | tf_op jit(solution)/shard_map/toeplitz/pallas_call | solution.py:33
  4.1 2.7 %copy.10 = bf16[2,64,8192]{2,1,0:T(8,128)(2,1)S(1)} copy(bf16[2,64,8192]{2,0,1:T(2,128)(2,1)} %bitcast.9) | data formatting | bytes 4194304 | tf_op jit(solution)/shard_map/transpose | solution.py:159
  7.1 1.1 %copy-done.2 = bf16[1280,512]{1,0:T(8,128)(2,1)S(1)} copy-done((bf16[1280,512]{1,0:T(8,128)(2,1)S(1)}, bf16[1280,512]{1,0:T(8,128)(2,1)}, u32[]{:S(2)}) %copy-start.2) | copy-done | bytes 1310744
  8.2 3.8 %compress.3 = bf16[16,128,256]{2,1,0:T(8,128)(2,1)} custom-call(bf16[128,9216]{1,0:T(8,128)(2,1)S(1)} %pad.10.x_ref, bf16[1280,512]{1,0:T(8,128)(2,1)S(1)} %copy-done.2), custom_call_target="tpu_custom_call" | custom-call | flops 2684354560 | bytes 2097152 | tf_op jit(solution)/shard_map/compress/pallas_call | solution.py:59
  12.0 6.6 %all-to-all-start.1 = ((bf16[16,128,256]{2,1,0:T(8,128)(2,1)}), bf16[16,128,256]{2,1,0:T(8,128)(2,1)S(1)}, u32[]{:S(2)}, u32[]{:S(2)}) async-start(bf16[16,128,256]{2,1,0:T(8,128)(2,1)} %compress.3), calls=%async_computation.1 | async-start | bytes 2097152 | tf_op jit(solution)/shard_map/all_to_all | solution.py:179
  18.6 1.3 %copy-done.3 = bf16[1280,512]{1,0:T(8,128)(2,1)S(1)} copy-done((bf16[1280,512]{1,0:T(8,128)(2,1)S(1)}, bf16[1280,512]{1,0:T(8,128)(2,1)}, u32[]{:S(2)}) %copy-start.3) | copy-done | bytes 1310744
  19.9 3.8 %compress.2 = bf16[16,128,256]{2,1,0:T(8,128)(2,1)} custom-call(bf16[128,9216]{1,0:T(8,128)(2,1)S(1)} %pad.10.x_ref, bf16[1280,512]{1,0:T(8,128)(2,1)S(1)} %copy-done.3), custom_call_target="tpu_custom_call" | custom-call | flops 2684354560 | bytes 2097152 | tf_op jit(solution)/shard_map/compress/pallas_call | solution.py:59
  23.8 19.7 %all-to-all-done.1.y_ref = bf16[16,128,256]{2,1,0:T(8,128)(2,1)S(1)} async-done(((bf16[16,128,256]{2,1,0:T(8,128)(2,1)}), bf16[16,128,256]{2,1,0:T(8,128)(2,1)S(1)}, u32[]{:S(2)}, u32[]{:S(2)}) %all-to-all-start.1) | async-done | bytes 1048608 | tf_op jit(solution)/shard_map/all_to_all | solution.py:179
  43.5 1.0 copy-done.6
  44.5 4.9 %all-to-all-start = ((bf16[16,128,256]{2,1,0:T(8,128)(2,1)}), bf16[16,128,256]{2,1,0:T(8,128)(2,1)S(1)}, u32[]{:S(2)}, u32[]{:S(2)}) async-start(bf16[16,128,256]{2,1,0:T(8,128)(2,1)} %compress.2), calls=%async_computation | async-start | bytes 2097152 | tf_op jit(solution)/shard_map/all_to_all | solution.py:179
  49.6 1.6 %copy-done.1 = bf16[1024,1024]{1,0:T(8,128)(2,1)S(1)} copy-done((bf16[1024,1024]{1,0:T(8,128)(2,1)S(1)}, bf16[1024,1024]{1,0:T(8,128)(2,1)}, u32[]{:S(2)}) %copy-start.1) | copy-done | bytes 2097176
  51.2 1.3 %spectra.1.g_ref = bf16[2,1024,32]{2,1,0:T(8,128)(2,1)S(1)} custom-call(bf16[1024,1024]{1,0:T(8,128)(2,1)S(1)} %copy-done.1, bf16[1024,1024]{1,0:T(8,128)(2,1)S(1)} %copy-done, bf16[2,512,16]{2,1,0:T(8,128)(2,1)S(1)} %bitcast.7), custom_call_target="tpu_custom_call" | custom-call | tf_op jit(solution)/shard_map/spectra/pallas_call | solution.py:162
  52.5 0.8 copy-done.4
  55.5 10.4 %azimuth.3 = (bf16[2,1024,256]{2,1,0:T(8,128)(2,1)}, f32[64,256]{1,0:T(8,128)}) custom-call(bf16[1024,1024]{1,0:T(8,128)(2,1)} %constant.33.clone.c_ref, bf16[1024,1024]{1,0:T(8,128)(2,1)} %constant.34.clone.s_ref, bf16[16,128,256]{2,1,0:T(8,128)(2,1)} %copy-done.6, bf16[2,1024,32]{2,1,0:T(8,128)(2,1)} %copy-done.4, s32[1,256]{1,0:T(1,128)} %bitcast.11, ...), custom_call_target="tpu_custom_call" | custom-call | flops 4294967296 | bytes 6291456 | tf_op jit(solution)/shard_map/azimuth/pallas_call | solution.py:120
  65.9 0.8 slice.14
  66.7 7.5 %all-to-all-done.y_ref = bf16[16,128,256]{2,1,0:T(8,128)(2,1)S(1)} async-done(((bf16[16,128,256]{2,1,0:T(8,128)(2,1)}), bf16[16,128,256]{2,1,0:T(8,128)(2,1)S(1)}, u32[]{:S(2)}, u32[]{:S(2)}) %all-to-all-start) | async-done | bytes 1048608 | tf_op jit(solution)/shard_map/all_to_all | solution.py:179
  74.3 1.0 copy-done.5
  75.2 10.5 %azimuth.2 = (bf16[2,1024,256]{2,1,0:T(8,128)(2,1)}, f32[64,256]{1,0:T(8,128)}) custom-call(bf16[1024,1024]{1,0:T(8,128)(2,1)} %constant.33.clone.c_ref, bf16[1024,1024]{1,0:T(8,128)(2,1)} %constant.34.clone.s_ref, bf16[16,128,256]{2,1,0:T(8,128)(2,1)} %copy-done.5, bf16[2,1024,32]{2,1,0:T(8,128)(2,1)} %copy-done.4, s32[1,256]{1,0:T(1,128)} %bitcast.10, ...), custom_call_target="tpu_custom_call" | custom-call | flops 4294967296 | bytes 6291456 | tf_op jit(solution)/shard_map/azimuth/pallas_call | solution.py:120
  86.5 2.1 %collective-permute-start.1 = (f32[64,16]{1,0:T(8,128)S(1)}, f32[64,16]{1,0:T(8,128)S(1)}, u32[]{:S(2)}, u32[]{:S(2)}) collective-permute-start(f32[64,16]{1,0:T(8,128)S(1)} %slice.15), channel_id=1, source_target_pairs={{1,0},{2,1},{3,2},{4,3},{5,4},{6,5},{7,6},{8,7},{9,8},{10,9},{11,1... | collective-permute-start | bytes 12296 | tf_op jit(solution)/shard_map/ppermute | solution.py:187
  88.6 4.6 %collective-permute-start = (f32[64,16]{1,0:T(8,128)S(1)}, f32[64,16]{1,0:T(8,128)S(1)}, u32[]{:S(2)}, u32[]{:S(2)}) collective-permute-start(f32[64,16]{1,0:T(8,128)S(1)} %slice.14), channel_id=1, source_target_pairs={{0,1},{1,2},{2,3},{3,4},{4,5},{5,6},{6,7},{7,8},{8,9},{9,10},{10,1... | collective-permute-start | bytes 12296 | tf_op jit(solution)/shard_map/ppermute | solution.py:186
  93.2 1.4 %maximum_bitcast_fusion = bf16[1024,2,512]{2,0,1:T(8,128)(2,1)S(1)} fusion(bf16[2,1024,256]{2,1,0:T(8,128)(2,1)S(1)} %copy-done.7, bf16[2,1024,256]{2,1,0:T(8,128)(2,1)} %get-tuple-element.6), kind=kLoop, calls=%fused_computation | loop fusion | flops 4194304 | bytes 4194304 | tf_op jit(solution)/shard_map/transpose | solution.py:184
  94.6 3.5 %copy.12 = bf16[1024,2,512]{2,1,0:T(2,128)(2,1)} copy(bf16[1024,2,512]{2,0,1:T(8,128)(2,1)S(1)} %maximum_bitcast_fusion) | data formatting | bytes 4194304
  98.1 1.1 %convolution_divide_fusion = f32[32,64]{1,0:T(8,128)} fusion(f32[64,16]{1,0:T(8,128)S(1)} %collective-permute-done.1, f32[64,256]{1,0:T(8,128)S(1)} %copy-done.9, f32[64,256]{1,0:T(8,128)S(1)} %copy-done.10, f32[64,16]{1,0:T(8,128)S(1)} %collective-permute-done, s32[32]{0:T(128)S(1)} %get-tuple-element.13, s32[32]{0:T(128)S(1)} %get-tuple-element.14, ...), kind=kOutput, calls=%fused_computation.1 | convolution fusion | flops 13547520 | bytes 150272 | tf_op jit(solution)/shard_map/ct,ic->ti/dot_general | solution.py:201
  (30 shorter events, 3.3 us)
Async XLA Ops:
  6.9 1.3 %copy-start.2 = (bf16[1280,512]{1,0:T(8,128)(2,1)S(1)}, bf16[1280,512]{1,0:T(8,128)(2,1)}, u32[]{:S(2)}) copy-start(bf16[1280,512]{1,0:T(8,128)(2,1)} %toeplitz.1.t_ref) | copy-start | bytes 3932164
  12.0 31.4 %all-to-all-start.1 = ((bf16[16,128,256]{2,1,0:T(8,128)(2,1)}), bf16[16,128,256]{2,1,0:T(8,128)(2,1)S(1)}, u32[]{:S(2)}, u32[]{:S(2)}) async-start(bf16[16,128,256]{2,1,0:T(8,128)(2,1)} %compress.3), calls=%async_computation.1 | async-start | bytes 2097152 | tf_op jit(solution)/shard_map/all_to_all | solution.py:179
  18.6 1.3 %copy-start.3 = (bf16[1280,512]{1,0:T(8,128)(2,1)S(1)}, bf16[1280,512]{1,0:T(8,128)(2,1)}, u32[]{:S(2)}) copy-start(bf16[1280,512]{1,0:T(8,128)(2,1)} %toeplitz.1.t_ref) | copy-start | bytes 3932164
  19.9 29.5 %copy-start.8 = (bf16[16,2,512]{2,1,0:T(2,128)(2,1)S(1)}, bf16[16,2,512]{2,1,0:T(2,128)(2,1)}, u32[]{:S(2)}) copy-start(bf16[16,2,512]{2,1,0:T(2,128)(2,1)} %param.10) | copy-start | bytes 98308
  23.8 25.8 %copy-start = (bf16[1024,1024]{1,0:T(8,128)(2,1)S(1)}, bf16[1024,1024]{1,0:T(8,128)(2,1)}, u32[]{:S(2)}) copy-start(bf16[1024,1024]{1,0:T(8,128)(2,1)} %constant.34.clone.s_ref) | copy-start | bytes 6291460
  43.5 1.0 copy-start.6
  44.5 29.8 %all-to-all-start = ((bf16[16,128,256]{2,1,0:T(8,128)(2,1)}), bf16[16,128,256]{2,1,0:T(8,128)(2,1)S(1)}, u32[]{:S(2)}, u32[]{:S(2)}) async-start(bf16[16,128,256]{2,1,0:T(8,128)(2,1)} %compress.2), calls=%async_computation | async-start | bytes 2097152 | tf_op jit(solution)/shard_map/all_to_all | solution.py:179
  49.6 1.6 %copy-start.1 = (bf16[1024,1024]{1,0:T(8,128)(2,1)S(1)}, bf16[1024,1024]{1,0:T(8,128)(2,1)}, u32[]{:S(2)}) copy-start(bf16[1024,1024]{1,0:T(8,128)(2,1)} %constant.33.clone.c_ref) | copy-start | bytes 6291460
  51.2 2.9 %copy-start.12 = (s32[64]{0:T(128)S(1)}, s32[64]{0:T(128)}, u32[]{:S(2)}) copy-start(s32[64]{0:T(128)} %param.12) | copy-start | bytes 772
  51.2 2.9 %copy-start.11 = (s32[512]{0:T(512)S(1)}, s32[512]{0:T(512)}, u32[]{:S(2)}) copy-start(s32[512]{0:T(512)} %param.11) | copy-start | bytes 6148
  52.5 0.8 copy-start.4
  74.3 1.0 copy-start.5
  75.2 18.0 %copy-start.7 = (bf16[2,1024,256]{2,1,0:T(8,128)(2,1)S(1)}, bf16[2,1024,256]{2,1,0:T(8,128)(2,1)}, u32[]{:S(2)}) copy-start(bf16[2,1024,256]{2,1,0:T(8,128)(2,1)} %get-tuple-element.7) | copy-start | bytes 3145732
  86.5 11.6 %collective-permute-start.1 = (f32[64,16]{1,0:T(8,128)S(1)}, f32[64,16]{1,0:T(8,128)S(1)}, u32[]{:S(2)}, u32[]{:S(2)}) collective-permute-start(f32[64,16]{1,0:T(8,128)S(1)} %slice.15), channel_id=1, source_target_pairs={{1,0},{2,1},{3,2},{4,3},{5,4},{6,5},{7,6},{8,7},{9,8},{10,9},{11,1... | collective-permute-start | bytes 12296 | tf_op jit(solution)/shard_map/ppermute | solution.py:187
  88.6 9.5 %collective-permute-start = (f32[64,16]{1,0:T(8,128)S(1)}, f32[64,16]{1,0:T(8,128)S(1)}, u32[]{:S(2)}, u32[]{:S(2)}) collective-permute-start(f32[64,16]{1,0:T(8,128)S(1)} %slice.14), channel_id=1, source_target_pairs={{0,1},{1,2},{2,3},{3,4},{4,5},{5,6},{6,7},{7,8},{8,9},{9,10},{10,1... | collective-permute-start | bytes 12296 | tf_op jit(solution)/shard_map/ppermute | solution.py:186
  94.6 3.5 %copy-start.9 = (f32[64,256]{1,0:T(8,128)S(1)}, f32[64,256]{1,0:T(8,128)}, u32[]{:S(2)}) copy-start(f32[64,256]{1,0:T(8,128)} %get-tuple-element.8) | copy-start | bytes 196612
  94.6 3.5 %copy-start.10 = (f32[64,256]{1,0:T(8,128)S(1)}, f32[64,256]{1,0:T(8,128)}, u32[]{:S(2)}) copy-start(f32[64,256]{1,0:T(8,128)} %get-tuple-element.9) | copy-start | bytes 196612
where the time goes:
time: 99.9 us; the launch traced here: 99.2 us
  Pallas kernels  32.2 us (32%)
  waiting for transfers between devices  27.2 us (27%)
  starting transfers between devices  18.2 us (18%)
  local copies, waits for them, and re-layouts  15.5 us (16%)
  other arithmetic  4.21 us (4%)
  matrix products  1.08 us (1%)
    all_to_all x2, waiting for transfers between devices, per_device(): lax.all_to_all(packed, 'row', split_axis=0, concat_axis=0, tiled=True)  27.2 us
    pallas_call x2, Pallas kernels, azimuth(): pl.pallas_call(azimuth_kernel, out_shape=(jax.ShapeDtypeStruct((2, pulses...  20.9 us
    all_to_all x2, starting transfers between devices, per_device(): lax.all_to_all(packed, 'row', split_axis=0, concat_axis=0, tiled=True)  11.5 us
    unnamed x28, local copies, waits for them, and re-layouts  10.4 us
    pallas_call x2, Pallas kernels, compress(): pl.pallas_call(functools.partial(compress_kernel, group, bins, start, wid...  7.69 us
    ppermute x1, starting transfers between devices, per_device(): lax.ppermute(sums[-1][:, width - EXT:], 'row', [(i, i + 1) for i in range...  4.56 us
    transpose x1, local copies, waits for them, and re-layouts, per_device(): rows = echoes.transpose(1, 0, 2).reshape(2 * local_pulses, samples)  2.75 us
    pallas_call x1, Pallas kernels, toeplitz(): pl.pallas_call(functools.partial(toeplitz_kernel, width), out_shape=jax.S...  2.2 us
  transfers between devices with their start and end apart: 4, of which 2 were waited for; matrix products, arithmetic and copies ran while one was open for 8% of the time, Pallas kernels for 16%

commit v1 on v0

v1 whole, which is shorter than its diff:
```python
import functools

import jax
import jax.numpy as jnp
import numpy as np
from jax import lax
from jax.experimental import pallas as pl
from jax.experimental.pallas import tpu as pltpu
from jax.sharding import PartitionSpec as P

TILE = 16
EXT = 16
HIGHEST = lax.Precision.HIGHEST
BF = jnp.bfloat16
F32 = jnp.float32


def mxu(left, right):
    return jnp.dot(left, right, preferred_element_type=F32)


def toeplitz_kernel(width, taps_ref, out_ref):
    for part in range(2):
        taps = jnp.broadcast_to(taps_ref[part : part + 1, :], (width, taps_ref.shape[1]))
        band = pltpu.roll(taps, 0, 1, stride=1, stride_axis=0)
        out_ref[:, part * width : (part + 1) * width] = band.T.astype(BF)


def toeplitz(range_replica, width):
    depth = range_replica.shape[1] + width
    taps = jnp.pad(range_replica.astype(F32), ((0, 0), (0, width)))
    return pl.pallas_call(
        functools.partial(toeplitz_kernel, width),
        out_shape=jax.ShapeDtypeStruct((depth, 2 * width), BF),
        name="toeplitz",
    )(taps)


def block(x_ref, t_ref, offsets):
    rows = x_ref.shape[0]
    half = rows // 2
    depth = t_ref.shape[0]
    width = t_ref.shape[1] // 2
    windows = [x_ref[:, pl.ds(offset, depth)] for offset in offsets]
    result = mxu(jnp.concatenate(windows, axis=0), t_ref[...])
    result = result.reshape(len(offsets), rows, 2 * width)
    real = result[:, :half, :width] + result[:, half:, width:]
    imag = result[:, half:, :width] - result[:, :half, width:]
    return jnp.concatenate([real, imag], axis=1).astype(BF)


def compress_kernel(group, bins, x_ref, t_ref, out_ref):
    step = pl.program_id(0)
    width = t_ref.shape[1] // 2
    for start in range(0, bins, width):
        offsets = [
            pl.multiple_of((step * group + i) * bins + start, 128) for i in range(group)
        ]
        out_ref[:, :, start : start + width] = block(x_ref, t_ref, offsets)


def exchange(x, bands, devices, bins):
    rows = x.shape[0]
    group = max(1, min(devices, 1024 // rows))
    packed = pl.pallas_call(
        functools.partial(compress_kernel, group, bins),
        grid=(devices // group,),
        in_specs=[
            pl.BlockSpec(x.shape, lambda g: (0, 0)),
            pl.BlockSpec(bands.shape, lambda g: (0, 0)),
        ],
        out_specs=pl.BlockSpec((group, rows, bins), lambda g: (g, 0, 0)),
        out_shape=jax.ShapeDtypeStruct((devices, rows, bins), BF),
        compiler_params=pltpu.CompilerParams(vmem_limit_bytes=48 * 2**20),
        name="compress",
    )(x, bands)
    return lax.all_to_all(packed, "row", split_axis=0, concat_axis=0, tiled=True)


def butterfly(parts, sign):
    radix = len(parts)
    if radix == 1:
        return parts
    (ar, ai), (br, bi), (cr, ci), (dr, di) = parts
    pr, pi, qr, qi = ar + cr, ai + ci, ar - cr, ai - ci
    tr, ti, ur, ui = br + dr, bi + di, br - dr, bi - di
    return [
        (pr + tr, pi + ti),
        (qr - sign * ui, qi + sign * ur),
        (pr - tr, pi - ti),
        (qr + sign * ui, qi - sign * ur),
    ]


def forward(table_ref, subsets, length):
    parts = []
    for j, (yr, yi) in enumerate(subsets):
        c, s = table_ref[j, 0, :, :length], table_ref[j, 1, :, :length]
        parts.append((mxu(c, yr) + mxu(s, yi), mxu(c, yi) - mxu(s, yr)))
    return butterfly(parts, -1.0)


def spectra_kernel(table_ref, g_ref, out_ref):
    radix, length = g_ref.shape[1], g_ref.shape[2]
    subsets = [(g_ref[0, j], g_ref[1, j]) for j in range(radix)]
    for m, pair in enumerate(forward(table_ref, subsets, length)):
        for part, value in enumerate(pair):
            high = value.astype(BF)
            low = (value - high.astype(F32)).astype(BF)
            out_ref[part, m] = jnp.concatenate([high, low], axis=1)


def azimuth_kernel(table_ref, back_ref, y_ref, g_ref, index_ref, mask_ref, out_ref, sums_ref):
    devices, rows, width = y_ref.shape
    radix, _, quarter, _ = table_ref.shape
    piece = rows // (2 * radix)

    def subset(k):
        return y_ref[:, k * piece : (k + 1) * piece, :].reshape(quarter, width)

    spectrum = forward(table_ref, [(subset(j), subset(radix + j)) for j in range(radix)], quarter)
    replicas = g_ref.shape[3] // 2
    which = lax.rem(lax.broadcasted_iota(jnp.int32, (2 * replicas, width), 0), replicas)
    pick = (which == index_ref[...]).astype(BF)
    scale = 1.0 / (radix * quarter)
    product = []
    for m, (fr, fi) in enumerate(spectrum):
        gr = mxu(g_ref[0, m], pick) * scale
        gi = mxu(g_ref[1, m], pick) * scale
        product.append((fr * gr + fi * gi, fi * gr - fr * gi))
    sums = jnp.zeros(sums_ref.shape, F32)
    for j, (zr, zi) in enumerate(butterfly(product, 1.0)):
        zr, zi = zr.astype(BF), zi.astype(BF)
        c, s = back_ref[j, 0], back_ref[j, 1]
        ar = mxu(c, zr) - mxu(s, zi)
        ai = mxu(c, zi) + mxu(s, zr)
        out_ref[0, j] = ar.astype(BF)
        out_ref[1, j] = ai.astype(BF)
        power = ar * ar + ai * ai
        high = power.astype(BF)
        low = (power - high.astype(F32)).astype(BF)
        mask = mask_ref[j]
        sums = sums + mxu(mask, high) + mxu(mask, low)
    sums_ref[...] = sums


def azimuth(table, back, y, spectra, index, mask, width):
    devices, rows, bins = y.shape
    radix, _, quarter, _ = table.shape
    return pl.pallas_call(
        azimuth_kernel,
        grid=(bins // width,),
        in_specs=[
            pl.BlockSpec(table.shape, lambda c: (0, 0, 0, 0)),
            pl.BlockSpec(back.shape, lambda c: (0, 0, 0, 0)),
            pl.BlockSpec((devices, rows, width), lambda c: (0, 0, c)),
            pl.BlockSpec(spectra.shape, lambda c: (0, 0, 0, 0)),
            pl.BlockSpec((1, width), lambda c: (0, c)),
            pl.BlockSpec(mask.shape, lambda c: (0, 0, 0)),
        ],
        out_specs=(
            pl.BlockSpec((2, radix, quarter, width), lambda c: (0, 0, 0, c)),
            pl.BlockSpec((mask.shape[1], width), lambda c: (0, c)),
        ),
        out_shape=(
            jax.ShapeDtypeStruct((2, radix, quarter, bins), BF),
            jax.ShapeDtypeStruct((mask.shape[1], bins), F32),
        ),
        compiler_params=pltpu.CompilerParams(vmem_limit_bytes=48 * 2**20),
        name="azimuth",
    )(table, back, y, spectra, index, mask)


def dft_tables(length, radix):
    quarter = length // radix
    freq = np.arange(quarter, dtype=np.int64)
    tables = []
    for j in range(radix):
        pulse = radix * np.arange(quarter, dtype=np.int64) + j
        angles = (np.outer(freq, pulse) % length) * (2.0 * np.pi / length)
        tables.append(np.stack([np.cos(angles), np.sin(angles)]))
    table = np.stack(tables)
    return jnp.asarray(table, dtype=BF), jnp.asarray(table.swapaxes(2, 3), dtype=BF)


def window_columns(positions, starts, stops):
    inside = (positions[:, None] >= starts[None, :]) & (positions[:, None] < stops[None, :])
    return inside.astype(F32)


def per_device(
    echoes, range_replica, azimuth_replicas, replica_index, azimuth_extent, range_extent
):
    devices = lax.axis_size("row")
    local_pulses, _, samples = echoes.shape
    taps = range_replica.shape[1]
    pulses = local_pulses * devices
    range_bins = samples // devices
    width = 256 if range_bins % 256 == 0 else 128
    radix = 4 if local_pulses % 64 == 0 else 1
    quarter = pulses // radix

    bands = toeplitz(range_replica, width)
    rows = echoes.reshape(local_pulses // radix, radix, 2, samples).transpose(2, 1, 0, 3)
    rows = jnp.pad(rows.reshape(2 * local_pulses, samples), ((0, 0), (0, taps)))
    table, back = dft_tables(pulses, radix)
    replicas, _, azimuth_taps = azimuth_replicas.shape
    split = azimuth_replicas.reshape(replicas, 2, azimuth_taps // radix, radix)
    spectra = pl.pallas_call(
        spectra_kernel,
        out_shape=jax.ShapeDtypeStruct((2, radix, quarter, 2 * replicas), BF),
        compiler_params=pltpu.CompilerParams(vmem_limit_bytes=48 * 2**20),
        name="spectra",
    )(table, split.transpose(1, 3, 2, 0))

    tile_rows = pulses // TILE
    pulse_start = jnp.arange(tile_rows, dtype=jnp.int32) * TILE - azimuth_extent
    pulse_stop = pulse_start + TILE + 2 * azimuth_extent
    order = jnp.arange(radix, dtype=jnp.int32)[:, None, None] + radix * jnp.arange(
        quarter, dtype=jnp.int32
    )
    pulse_mask = (order >= pulse_start[:, None]) & (order < pulse_stop[:, None])
    pulse_count = (jnp.minimum(pulse_stop, pulses) - jnp.maximum(pulse_start, 0)).astype(F32)
    pulse_mask = pulse_mask.astype(BF)

    turned = exchange(rows, bands, devices, range_bins)
    index = replica_index.reshape(1, range_bins)
    image, sums = azimuth(table, back, turned, spectra, index, pulse_mask, width)
    focused = image.transpose(2, 1, 0, 3).reshape(pulses, 2, range_bins)
    ends = devices - 1
    before = lax.ppermute(sums[:, range_bins - EXT :], "row", [(i, i + 1) for i in range(ends)])
    after = lax.ppermute(sums[:, :EXT], "row", [(i + 1, i) for i in range(ends)])
    row_sums = jnp.concatenate([before, sums, after], axis=1)

    local_tiles = range_bins // TILE
    device = lax.axis_index("row")
    tile_ids = device * local_tiles + jnp.arange(local_tiles, dtype=jnp.int32)
    local_extent = lax.dynamic_slice_in_dim(range_extent, device * local_tiles, local_tiles)
    range_start = tile_ids * TILE - local_extent
    range_stop = range_start + TILE + 2 * local_extent
    range_count = (
        jnp.minimum(range_stop, samples) - jnp.maximum(range_start, 0)
    ).astype(F32)
    positions = device * range_bins - EXT + jnp.arange(range_bins + 2 * EXT, dtype=jnp.int32)
    range_mask = window_columns(positions, range_start, range_stop)
    window_sums = jnp.einsum(
        "ct,ic->ti", range_mask, row_sums, precision=HIGHEST, preferred_element_type=F32
    )
    looked = window_sums / (range_count[:, None] * pulse_count[None, :])
    return (focused, looked)


def solution(mesh):
    return jax.shard_map(
        per_device,
        mesh=mesh,
        in_specs=(
            P(("scene", "row"), None, None),
            P(),
            P(),
            P(("scene", "row")),
            P("scene"),
            P("scene"),
        ),
        out_specs=(P("scene", None, "row"), P(("scene", "row"), None)),
        check_vma=False,
    )
```

time: 99.9 us -> 87.4 us (0.87)
  waiting for transfers between devices: 27.2 us -> 46.4 us
  Pallas kernels: 32.2 us -> 16.3 us
  local copies, waits for them, and re-layouts: 15.5 us -> 7.86 us
  starting transfers between devices: 18.2 us -> 13.1 us
  other arithmetic: 4.21 us -> 1.5 us
    all_to_all x2 -> x1, waiting for transfers between devices: 27.2 us -> 46.4 us  [exchange(): lax.all_to_all(packed, 'row', split_axis=0, concat_axis=0, tiled=True)]
    pallas_call x5 -> x3, Pallas kernels: 30 us -> 14.1 us  [the longest x1 6.72 us: exchange(): pl.pallas_call(functools.partial(compress_kernel, group, bins), grid=(dev...]
    unnamed x28 -> x15, local copies, waits for them, and re-layouts: 10.4 us -> 1.32 us
    all_to_all x2 -> x1, starting transfers between devices: 11.5 us -> 6.69 us  [exchange(): lax.all_to_all(packed, 'row', split_axis=0, concat_axis=0, tiled=True)]
    reshape x0 -> x2, local copies, waits for them, and re-layouts: none -> 2.79 us  [the longest x1 2.76 us: per_device(): echoes.reshape(local_pulses // radix, radix, 2, samples)]
    slice x3 -> x1, local copies, waits for them, and re-layouts: 2.19 us -> 0.08 us  [per_device(): sums[:, range_bins - EXT:]]
    transpose x1 -> x0, other arithmetic: 1.39 us -> none  [per_device(): focused = jnp.concatenate(images, axis=2).transpose(1, 0, 2)]
  transfers between devices with their start and end apart: 4 -> 3, of which waited for: 2 -> 1; matrix products, arithmetic and copies ran while one was open for 8% -> 5% of each run, Pallas kernels for 16% -> 1%
where the time goes in v1:
time: 87.4 us; the launch traced here: 87 us
  waiting for transfers between devices  46.4 us (53%)
  Pallas kernels  16.3 us (19%)
  starting transfers between devices  13.1 us (15%)
  local copies, waits for them, and re-layouts  7.86 us (9%)
  other arithmetic  1.5 us (2%)
  matrix products  1.07 us (1%)
    all_to_all x1, waiting for transfers between devices, exchange(): lax.all_to_all(packed, 'row', split_axis=0, concat_axis=0, tiled=True)  46.4 us
    pallas_call x1, Pallas kernels, exchange(): pl.pallas_call(functools.partial(compress_kernel, group, bins), grid=(dev...  6.72 us
    pallas_call x1, Pallas kernels, azimuth(): pl.pallas_call(azimuth_kernel, grid=(bins // width,), in_specs=[pl.BlockS...  6.69 us
    all_to_all x1, starting transfers between devices, exchange(): lax.all_to_all(packed, 'row', split_axis=0, concat_axis=0, tiled=True)  6.69 us
    ppermute x1, starting transfers between devices, per_device(): lax.ppermute(sums[:, range_bins - EXT:], 'row', [(i, i + 1) for i in rang...  4.34 us
    transpose x1, local copies, waits for them, and re-layouts, per_device(): focused = image.transpose(2, 1, 0, 3).reshape(pulses, 2, range_bins)  3.47 us
    reshape x1, local copies, waits for them, and re-layouts, per_device(): echoes.reshape(local_pulses // radix, radix, 2, samples)  2.76 us
    pallas_call x1, Pallas kernels, toeplitz(): pl.pallas_call(functools.partial(toeplitz_kernel, width), out_shape=jax.S...  2.2 us
  transfers between devices with their start and end apart: 3, of which 1 were waited for; matrix products, arithmetic and copies ran while one was open for 5% of the time, Pallas kernels for 1%

profile of v1, /device:TPU:15, one launch (start us, length us, event | category | flops | bytes accessed | tf_op | source)
XLA Modules:
  0.0 87.0 jit_solution(17616210063192802910)
XLA Ops:
  0.6 0.0 copy-start.5
  0.6 2.8 %copy.11 = bf16[16,4,2,8192]{3,0,1,2:T(8,128)(2,1)S(1)} copy(bf16[16,4,2,8192]{3,2,1,0:T(2,128)(2,1)} %bitcast.15) | data formatting | bytes 4194304 | tf_op jit(solution)/shard_map/reshape | solution.py:204
  3.4 0.0 copy-done.5
  3.4 0.6 pad_convert_fusion.taps_ref
  4.0 2.2 %toeplitz.1.t_ref = bf16[1280,512]{1,0:T(8,128)(2,1)} custom-call(f32[2,1280]{1,0:T(2,128)} %pad_convert_fusion.taps_ref), custom_call_target="tpu_custom_call" | custom-call | tf_op jit(solution)/shard_map/toeplitz/pallas_call | solution.py:32
  6.2 0.2 pad.10.x_ref
  6.4 1.1 %copy-done = bf16[1280,512]{1,0:T(8,128)(2,1)S(1)} copy-done((bf16[1280,512]{1,0:T(8,128)(2,1)S(1)}, bf16[1280,512]{1,0:T(8,128)(2,1)}, u32[]{:S(2)}) %copy-start) | copy-done | bytes 1310744
  7.5 6.7 %compress.1 = bf16[16,128,512]{2,1,0:T(8,128)(2,1)} custom-call(bf16[128,9216]{1,0:T(8,128)(2,1)S(1)} %pad.10.x_ref, bf16[1280,512]{1,0:T(8,128)(2,1)S(1)} %copy-done), custom_call_target="tpu_custom_call" | custom-call | tf_op jit(solution)/shard_map/compress/pallas_call | solution.py:65
  14.3 6.7 %all-to-all-start = ((bf16[16,128,512]{2,1,0:T(8,128)(2,1)}), bf16[16,128,512]{2,1,0:T(8,128)(2,1)}, u32[]{:S(2)}, u32[]{:S(2)}) async-start(bf16[16,128,512]{2,1,0:T(8,128)(2,1)} %compress.1), calls=%async_computation | async-start | bytes 4194304 | tf_op jit(solution)/shard_map/all_to_all | solution.py:77
  21.0 0.0 copy-start.2
  21.0 0.0 copy-start.3
  21.0 0.2 copy.12
  21.2 0.7 spectra.1.g_ref
  22.0 0.1 and_convert_fusion.1.mask_ref
  22.1 46.4 %all-to-all-done.y_ref = bf16[16,128,512]{2,1,0:T(8,128)(2,1)} async-done(((bf16[16,128,512]{2,1,0:T(8,128)(2,1)}), bf16[16,128,512]{2,1,0:T(8,128)(2,1)}, u32[]{:S(2)}, u32[]{:S(2)}) %all-to-all-start) | async-done | bytes 2097184 | tf_op jit(solution)/shard_map/all_to_all | solution.py:77
  68.5 6.7 %azimuth.1 = (bf16[2,4,256,512]{3,2,1,0:T(8,128)(2,1)S(1)}, f32[64,512]{1,0:T(8,128)S(1)}) custom-call(bf16[4,2,256,256]{3,2,1,0:T(8,128)(2,1)S(1)} %copy-done.1, bf16[4,2,256,256]{3,2,1,0:T(8,128)(2,1)S(1)} %copy-done.2, bf16[16,128,512]{2,1,0:T(8,128)(2,1)} %all-to-all-done.y_ref, bf16[2,4,256,32]{3,2,1,0:T(8,128)(2,1)S(1)} %spectra.1.g_ref, ...), custom_call_target="tpu_custom_call" | custom-call | tf_op jit(solution)/shard_map/azimuth/pallas_call | solution.py:150
  75.2 0.1 fusion.9
  75.3 2.1 %collective-permute-start.1 = (f32[64,16]{1,0:T(8,128)S(1)}, f32[64,16]{1,0:T(8,128)S(1)}, u32[]{:S(2)}, u32[]{:S(2)}) collective-permute-start(f32[64,16]{1,0:T(8,128)S(1)} %get-tuple-element.10), channel_id=1, source_target_pairs={{1,0},{2,1},{3,2},{4,3},{5,4},{6,5},{7,6},{8,7},{9,8},{10,9},{11,1... | collective-permute-start | bytes 12296 | tf_op jit(solution)/shard_map/ppermute | solution.py:232
  77.4 4.3 %collective-permute-start = (f32[64,16]{1,0:T(8,128)S(1)}, f32[64,16]{1,0:T(8,128)S(1)}, u32[]{:S(2)}, u32[]{:S(2)}) collective-permute-start(f32[64,16]{1,0:T(8,128)S(1)} %get-tuple-element.9), channel_id=1, source_target_pairs={{0,1},{1,2},{2,3},{3,4},{4,5},{5,6},{6,7},{7,8},{8,9},{9,10},{10,1... | collective-permute-start | bytes 12296 | tf_op jit(solution)/shard_map/ppermute | solution.py:231
  81.7 0.8 subtract_convert_fusion.1
  82.5 3.5 %copy.14 = bf16[256,4,2,512]{3,2,1,0:T(2,128)(2,1)} copy(bf16[256,4,2,512]{3,0,1,2:T(8,128)(2,1)S(1)} %bitcast.11) | data formatting | bytes 4194304 | tf_op jit(solution)/shard_map/transpose | solution.py:229
  86.0 0.0 collective-permute-done.1
  86.0 0.0 collective-permute-done
  86.0 1.1 %convolution_divide_fusion = f32[32,64]{1,0:T(8,128)} fusion(f32[64,16]{1,0:T(8,128)S(1)} %collective-permute-done.1, f32[64,512]{1,0:T(8,128)S(1)} %get-tuple-element.5, f32[64,16]{1,0:T(8,128)S(1)} %collective-permute-done, s32[32]{0:T(128)S(1)} %get-tuple-element.7, s32[32]{0:T(128)S(1)} %get-tuple-element.8, s32[544]{0:T(1024)S(1)} %iota_add_fusion, ...), kind=kOutput, calls=%fused_computation | convolution fusion | flops 13512704 | bytes 150272 | tf_op jit(solution)/shard_map/ct,ic->ti/dot_general | solution.py:246
  (14 shorter events, 0.1 us)
Async XLA Ops:
  0.6 2.8 %copy-start.5 = (bf16[2,1024]{1,0:T(2,128)(2,1)S(1)}, bf16[2,1024]{1,0:T(2,128)(2,1)}, u32[]{:S(2)}) copy-start(bf16[2,1024]{1,0:T(2,128)(2,1)} %param.9) | copy-start | bytes 12292
  6.2 1.3 %copy-start = (bf16[1280,512]{1,0:T(8,128)(2,1)S(1)}, bf16[1280,512]{1,0:T(8,128)(2,1)}, u32[]{:S(2)}) copy-start(bf16[1280,512]{1,0:T(8,128)(2,1)} %toeplitz.1.t_ref) | copy-start | bytes 3932164
  14.3 6.7 %copy-start.4 = (bf16[16,2,512]{2,1,0:T(2,128)(2,1)S(1)}, bf16[16,2,512]{2,1,0:T(2,128)(2,1)}, u32[]{:S(2)}) copy-start(bf16[16,2,512]{2,1,0:T(2,128)(2,1)} %param.10) | copy-start | bytes 98308
  14.3 7.0 %copy-start.1 = (bf16[4,2,256,256]{3,2,1,0:T(8,128)(2,1)S(1)}, bf16[4,2,256,256]{3,2,1,0:T(8,128)(2,1)}, u32[]{:S(2)}) copy-start(bf16[4,2,256,256]{3,2,1,0:T(8,128)(2,1)} %constant.35.clone.table_ref) | copy-start | bytes 3145732
  14.3 54.2 %all-to-all-start = ((bf16[16,128,512]{2,1,0:T(8,128)(2,1)}), bf16[16,128,512]{2,1,0:T(8,128)(2,1)}, u32[]{:S(2)}, u32[]{:S(2)}) async-start(bf16[16,128,512]{2,1,0:T(8,128)(2,1)} %compress.1), calls=%async_computation | async-start | bytes 4194304 | tf_op jit(solution)/shard_map/all_to_all | solution.py:77
  20.9 1.0 %copy-start.6 = (s32[64]{0:T(128)S(1)}, s32[64]{0:T(128)}, u32[]{:S(2)}) copy-start(s32[64]{0:T(128)} %param.12) | copy-start | bytes 772
  21.0 47.5 %copy-start.2 = (bf16[4,2,256,256]{3,2,1,0:T(8,128)(2,1)S(1)}, bf16[4,2,256,256]{3,2,1,0:T(8,128)(2,1)}, u32[]{:S(2)}) copy-start(bf16[4,2,256,256]{3,2,1,0:T(8,128)(2,1)} %constant.36.clone.back_ref) | copy-start | bytes 3145732
  21.0 47.5 %copy-start.3 = (s32[512]{0:T(512)S(1)}, s32[512]{0:T(512)}, u32[]{:S(2)}) copy-start(s32[512]{0:T(512)} %param.11) | copy-start | bytes 6148
  75.3 10.7 %collective-permute-start.1 = (f32[64,16]{1,0:T(8,128)S(1)}, f32[64,16]{1,0:T(8,128)S(1)}, u32[]{:S(2)}, u32[]{:S(2)}) collective-permute-start(f32[64,16]{1,0:T(8,128)S(1)} %get-tuple-element.10), channel_id=1, source_target_pairs={{1,0},{2,1},{3,2},{4,3},{5,4},{6,5},{7,6},{8,7},{9,8},{10,9},{11,1... | collective-permute-start | bytes 12296 | tf_op jit(solution)/shard_map/ppermute | solution.py:232
  77.4 8.6 %collective-permute-start = (f32[64,16]{1,0:T(8,128)S(1)}, f32[64,16]{1,0:T(8,128)S(1)}, u32[]{:S(2)}, u32[]{:S(2)}) collective-permute-start(f32[64,16]{1,0:T(8,128)S(1)} %get-tuple-element.9), channel_id=1, source_target_pairs={{0,1},{1,2},{2,3},{3,4},{4,5},{5,6},{6,7},{7,8},{8,9},{9,10},{10,1... | collective-permute-start | bytes 12296 | tf_op jit(solution)/shard_map/ppermute | solution.py:231

commit v2 on v1

--- a/solution.py
+++ b/solution.py
@@ -49,32 +49,76 @@
     return jnp.concatenate([real, imag], axis=1).astype(BF)
 
 
-def compress_kernel(group, bins, x_ref, t_ref, out_ref):
-    step = pl.program_id(0)
+def exchange_kernel(devices, bins, x_ref, t_ref, out_ref, packed, send_sems, recv_sems, own_sem):
+    me = lax.axis_index("row")
     width = t_ref.shape[1] // 2
-    for start in range(0, bins, width):
-        offsets = [
-            pl.multiple_of((step * group + i) * bins + start, 128) for i in range(group)
-        ]
-        out_ref[:, :, start : start + width] = block(x_ref, t_ref, offsets)
+    barrier = pltpu.get_barrier_semaphore()
+
+    def greet(i, carry):
+        pl.semaphore_signal(
+            barrier,
+            inc=1,
+            device_id={"row": lax.rem(me + i, devices)},
+            device_id_type=pl.DeviceIdType.MESH,
+        )
+        return carry
+
+    lax.fori_loop(1, devices, greet, 0)
+
+    def fill(target):
+        for start in range(0, bins, width):
+            offset = pl.multiple_of(target * bins + start, 128)
+            packed[target, :, start : start + width] = block(x_ref, t_ref, [offset])[0]
+
+    def remote(i):
+        target = lax.rem(me + i, devices)
+        return pltpu.make_async_remote_copy(
+            src_ref=packed.at[target],
+            dst_ref=out_ref.at[me],
+            send_sem=send_sems.at[i],
+            recv_sem=recv_sems.at[i],
+            device_id={"row": target},
+            device_id_type=pl.DeviceIdType.MESH,
+        )
+
+    fill(lax.rem(me + 1, devices))
+    pl.semaphore_wait(barrier, devices - 1)
+
+    def step(i, carry):
+        remote(i).start()
+        fill(lax.rem(me + i + 1, devices))
+        return carry
+
+    lax.fori_loop(1, devices, step, 0)
+    own = pltpu.make_async_copy(packed.at[me], out_ref.at[me], own_sem)
+    own.start()
+
+    def finish(i, carry):
+        remote(i).wait()
+        return carry
+
+    lax.fori_loop(1, devices, finish, 0)
+    own.wait()
 
 
 def exchange(x, bands, devices, bins):
     rows = x.shape[0]
-    group = max(1, min(devices, 1024 // rows))
-    packed = pl.pallas_call(
-        functools.partial(compress_kernel, group, bins),
-        grid=(devices // group,),
-        in_specs=[
-            pl.BlockSpec(x.shape, lambda g: (0, 0)),
-            pl.BlockSpec(bands.shape, lambda g: (0, 0)),
+    return pl.pallas_call(
+        functools.partial(exchange_kernel, devices, bins),
+        in_specs=[pl.BlockSpec(memory_space=pltpu.VMEM)] * 2,
+        out_specs=pl.BlockSpec(memory_space=pl.ANY),
+        out_shape=jax.ShapeDtypeStruct((devices, rows, bins), BF),
+        scratch_shapes=[
+            pltpu.VMEM((devices, rows, bins), BF),
+            pltpu.SemaphoreType.DMA((devices,)),
+            pltpu.SemaphoreType.DMA((devices,)),
+            pltpu.SemaphoreType.DMA,
         ],
-        out_specs=pl.BlockSpec((group, rows, bins), lambda g: (g, 0, 0)),
-        out_shape=jax.ShapeDtypeStruct((devices, rows, bins), BF),
-        compiler_params=pltpu.CompilerParams(vmem_limit_bytes=48 * 2**20),
-        name="compress",
+        compiler_params=pltpu.CompilerParams(
+            collective_id=0, has_side_effects=True, vmem_limit_bytes=48 * 2**20
+        ),
+        name="exchange",
     )(x, bands)
-    return lax.all_to_all(packed, "row", split_axis=0, concat_axis=0, tiled=True)
 
 
 def butterfly(parts, sign):

time: 87.4 us -> 81 us (0.927)
  waiting for transfers between devices: 46.4 us -> 0.01 us
  Pallas kernels: 16.3 us -> 61.2 us
  starting transfers between devices: 13.1 us -> 6.45 us
  local copies, waits for them, and re-layouts: 7.86 us -> 9.57 us
    all_to_all x1 -> x0, waiting for transfers between devices: 46.4 us -> none  [exchange(): lax.all_to_all(packed, 'row', split_axis=0, concat_axis=0, tiled=True)]
    pallas_call x1, Pallas kernels: 6.72 us -> 51.5 us  [exchange(): pl.pallas_call(functools.partial(exchange_kernel, devices, bins), in_spec...]
    all_to_all x1 -> x0, starting transfers between devices: 6.69 us -> none  [exchange(): lax.all_to_all(packed, 'row', split_axis=0, concat_axis=0, tiled=True)]
    unnamed x15 -> x17, local copies, waits for them, and re-layouts: 1.32 us -> 3.02 us
  transfers between devices with their start and end apart: 3 -> 2, of which waited for: 1 -> 0; matrix products, arithmetic and copies ran while one was open for 5% -> 5% of each run, Pallas kernels for 1% -> 0%
where the time goes in v2:
time: 81 us; the launch traced here: 80.6 us
  Pallas kernels  61.2 us (76%)
  local copies, waits for them, and re-layouts  9.57 us (12%)
  starting transfers between devices  6.45 us (8%)
  other arithmetic  1.5 us (2%)
  matrix products  1.07 us (1%)
  between operations  0.81 us (1%)
    pallas_call x1, Pallas kernels, exchange(): pl.pallas_call(functools.partial(exchange_kernel, devices, bins), in_spec...  51.5 us
    pallas_call x1, Pallas kernels, azimuth(): pl.pallas_call(azimuth_kernel, grid=(bins // width,), in_specs=[pl.BlockS...  6.79 us
    ppermute x1, starting transfers between devices, per_device(): lax.ppermute(sums[:, range_bins - EXT:], 'row', [(i, i + 1) for i in rang...  4.54 us
    transpose x1, local copies, waits for them, and re-layouts, per_device(): focused = image.transpose(2, 1, 0, 3).reshape(pulses, 2, range_bins)  3.47 us
    unnamed x17, local copies, waits for them, and re-layouts  3.02 us
    reshape x1, local copies, waits for them, and re-layouts, per_device(): echoes.reshape(local_pulses // radix, radix, 2, samples)  2.76 us
    pallas_call x1, Pallas kernels, toeplitz(): pl.pallas_call(functools.partial(toeplitz_kernel, width), out_shape=jax.S...  2.2 us
    ppermute x1, starting transfers between devices, per_device(): lax.ppermute(sums[:, :EXT], 'row', [(i + 1, i) for i in range(ends)])  1.91 us
  transfers between devices with their start and end apart: 2, of which 0 were waited for; matrix products, arithmetic and copies ran while one was open for 5% of the time, Pallas kernels for 0%

profile of v2, /device:TPU:15, one launch (start us, length us, event | category | flops | bytes accessed | tf_op | source)
XLA Modules:
  0.0 80.6 jit_solution(18239656891232774239)
XLA Ops:
  0.6 0.0 copy-start.6
  0.7 0.0 copy-start.5
  0.7 2.8 %copy.11 = bf16[16,4,2,8192]{3,0,1,2:T(8,128)(2,1)S(1)} copy(bf16[16,4,2,8192]{3,2,1,0:T(2,128)(2,1)} %bitcast.15) | data formatting | bytes 4194304 | tf_op jit(solution)/shard_map/reshape | solution.py:248
  3.4 0.0 copy-start.7
  3.5 0.6 pad_convert_fusion.taps_ref
  4.1 2.2 %toeplitz.1.t_ref = bf16[1280,512]{1,0:T(8,128)(2,1)} custom-call(f32[2,1280]{1,0:T(2,128)} %pad_convert_fusion.taps_ref), custom_call_target="tpu_custom_call" | custom-call | tf_op jit(solution)/shard_map/toeplitz/pallas_call | solution.py:32
  6.3 0.2 copy.12
  6.5 0.0 copy-start.1
  6.5 0.2 pad.10.x_ref
  6.8 1.1 %copy-done.1 = bf16[1280,512]{1,0:T(8,128)(2,1)S(1)} copy-done((bf16[1280,512]{1,0:T(8,128)(2,1)S(1)}, bf16[1280,512]{1,0:T(8,128)(2,1)}, u32[]{:S(2)}) %copy-start.1) | copy-done | bytes 1310744
  7.9 51.5 %exchange.1.y_ref = bf16[16,128,512]{2,1,0:T(8,128)(2,1)S(1)} custom-call(bf16[128,9216]{1,0:T(8,128)(2,1)S(1)} %pad.10.x_ref, bf16[1280,512]{1,0:T(8,128)(2,1)S(1)} %copy-done.1), custom_call_target="tpu_custom_call" | custom-call | tf_op jit(solution)/shard_map/exchange/pallas_call | solution.py:106
  59.4 0.0 copy-start
  59.4 1.3 %copy-done = bf16[16,128,512]{2,1,0:T(8,128)(2,1)} copy-done((bf16[16,128,512]{2,1,0:T(8,128)(2,1)}, bf16[16,128,512]{2,1,0:T(8,128)(2,1)S(1)}, u32[]{:S(2)}) %copy-start) | copy-done | bytes 2097176
  60.7 0.7 spectra.1.g_ref
  61.4 0.1 and_convert_fusion.1.mask_ref
  61.5 0.4 copy-done.3
  61.9 6.8 %azimuth.1 = (bf16[2,4,256,512]{3,2,1,0:T(8,128)(2,1)S(1)}, f32[64,512]{1,0:T(8,128)S(1)}) custom-call(bf16[4,2,256,256]{3,2,1,0:T(8,128)(2,1)S(1)} %copy-done.2, bf16[4,2,256,256]{3,2,1,0:T(8,128)(2,1)S(1)} %copy-done.3, bf16[16,128,512]{2,1,0:T(8,128)(2,1)} %copy-done, bf16[2,4,256,32]{3,2,1,0:T(8,128)(2,1)S(1)} %spectra.1.g_ref, s32[1,512]{1,0:T(1,128)S(1)} %bitcast.13, ...), custom_call_target="tpu_custom_call" | custom-call | tf_op jit(solution)/shard_map/azimuth/pallas_call | solution.py:194
  68.7 0.1 fusion.9
  68.8 1.9 %collective-permute-start.1 = (f32[64,16]{1,0:T(8,128)S(1)}, f32[64,16]{1,0:T(8,128)S(1)}, u32[]{:S(2)}, u32[]{:S(2)}) collective-permute-start(f32[64,16]{1,0:T(8,128)S(1)} %get-tuple-element.10), channel_id=1, source_target_pairs={{1,0},{2,1},{3,2},{4,3},{5,4},{6,5},{7,6},{8,7},{9,8},{10,9},{11,1... | collective-permute-start | bytes 12296 | tf_op jit(solution)/shard_map/ppermute | solution.py:276
  70.7 4.5 %collective-permute-start = (f32[64,16]{1,0:T(8,128)S(1)}, f32[64,16]{1,0:T(8,128)S(1)}, u32[]{:S(2)}, u32[]{:S(2)}) collective-permute-start(f32[64,16]{1,0:T(8,128)S(1)} %get-tuple-element.9), channel_id=1, source_target_pairs={{0,1},{1,2},{2,3},{3,4},{4,5},{5,6},{6,7},{7,8},{8,9},{9,10},{10,1... | collective-permute-start | bytes 12296 | tf_op jit(solution)/shard_map/ppermute | solution.py:275
  75.3 0.8 subtract_convert_fusion.1
  76.1 3.5 %copy.14 = bf16[256,4,2,512]{3,2,1,0:T(2,128)(2,1)} copy(bf16[256,4,2,512]{3,0,1,2:T(8,128)(2,1)S(1)} %bitcast.11) | data formatting | bytes 4194304 | tf_op jit(solution)/shard_map/transpose | solution.py:273
  79.6 0.0 collective-permute-done.1
  79.6 1.1 %convolution_divide_fusion = f32[32,64]{1,0:T(8,128)} fusion(f32[64,16]{1,0:T(8,128)S(1)} %collective-permute-done.1, f32[64,512]{1,0:T(8,128)S(1)} %get-tuple-element.5, f32[64,16]{1,0:T(8,128)S(1)} %collective-permute-done, s32[32]{0:T(128)S(1)} %get-tuple-element.7, s32[32]{0:T(128)S(1)} %get-tuple-element.8, s32[544]{0:T(1024)S(1)} %iota_add_fusion, ...), kind=kOutput, calls=%fused_computation | convolution fusion | flops 13512704 | bytes 150272 | tf_op jit(solution)/shard_map/ct,ic->ti/dot_general | solution.py:290
  (14 shorter events, 0.1 us)
Async XLA Ops:
  0.6 2.8 %copy-start.6 = (bf16[2,1024]{1,0:T(2,128)(2,1)S(1)}, bf16[2,1024]{1,0:T(2,128)(2,1)}, u32[]{:S(2)}) copy-start(bf16[2,1024]{1,0:T(2,128)(2,1)} %param.9) | copy-start | bytes 12292
  0.7 5.6 %copy-start.5 = (bf16[16,2,512]{2,1,0:T(2,128)(2,1)S(1)}, bf16[16,2,512]{2,1,0:T(2,128)(2,1)}, u32[]{:S(2)}) copy-start(bf16[16,2,512]{2,1,0:T(2,128)(2,1)} %param.10) | copy-start | bytes 98308
  3.4 3.1 %copy-start.7 = (s32[64]{0:T(128)S(1)}, s32[64]{0:T(128)}, u32[]{:S(2)}) copy-start(s32[64]{0:T(128)} %param.12) | copy-start | bytes 772
  6.5 1.3 %copy-start.1 = (bf16[1280,512]{1,0:T(8,128)(2,1)S(1)}, bf16[1280,512]{1,0:T(8,128)(2,1)}, u32[]{:S(2)}) copy-start(bf16[1280,512]{1,0:T(8,128)(2,1)} %toeplitz.1.t_ref) | copy-start | bytes 3932164
  7.9 52.9 %copy-start.2 = (bf16[4,2,256,256]{3,2,1,0:T(8,128)(2,1)S(1)}, bf16[4,2,256,256]{3,2,1,0:T(8,128)(2,1)}, u32[]{:S(2)}) copy-start(bf16[4,2,256,256]{3,2,1,0:T(8,128)(2,1)} %constant.35.clone.table_ref) | copy-start | bytes 3145732
  7.9 53.7 %copy-start.4 = (s32[512]{0:T(512)S(1)}, s32[512]{0:T(512)}, u32[]{:S(2)}) copy-start(s32[512]{0:T(512)} %param.11) | copy-start | bytes 6148
  59.4 1.3 %copy-start = (bf16[16,128,512]{2,1,0:T(8,128)(2,1)}, bf16[16,128,512]{2,1,0:T(8,128)(2,1)S(1)}, u32[]{:S(2)}) copy-start(bf16[16,128,512]{2,1,0:T(8,128)(2,1)S(1)} %exchange.1.y_ref) | copy-start | bytes 6291460
  60.7 1.2 %copy-start.3 = (bf16[4,2,256,256]{3,2,1,0:T(8,128)(2,1)S(1)}, bf16[4,2,256,256]{3,2,1,0:T(8,128)(2,1)}, u32[]{:S(2)}) copy-start(bf16[4,2,256,256]{3,2,1,0:T(8,128)(2,1)} %constant.36.clone.back_ref) | copy-start | bytes 3145732
  68.8 10.7 %collective-permute-start.1 = (f32[64,16]{1,0:T(8,128)S(1)}, f32[64,16]{1,0:T(8,128)S(1)}, u32[]{:S(2)}, u32[]{:S(2)}) collective-permute-start(f32[64,16]{1,0:T(8,128)S(1)} %get-tuple-element.10), channel_id=1, source_target_pairs={{1,0},{2,1},{3,2},{4,3},{5,4},{6,5},{7,6},{8,7},{9,8},{10,9},{11,1... | collective-permute-start | bytes 12296 | tf_op jit(solution)/shard_map/ppermute | solution.py:276
  70.7 8.8 %collective-permute-start = (f32[64,16]{1,0:T(8,128)S(1)}, f32[64,16]{1,0:T(8,128)S(1)}, u32[]{:S(2)}, u32[]{:S(2)}) collective-permute-start(f32[64,16]{1,0:T(8,128)S(1)} %get-tuple-element.9), channel_id=1, source_target_pairs={{0,1},{1,2},{2,3},{3,4},{4,5},{5,6},{6,7},{7,8},{8,9},{9,10},{10,1... | collective-permute-start | bytes 12296 | tf_op jit(solution)/shard_map/ppermute | solution.py:275

commit v3 on v1

v3 whole, which is shorter than its diff:
```python
import functools

import jax
import jax.numpy as jnp
import numpy as np
from jax import lax
from jax.experimental import pallas as pl
from jax.experimental.pallas import tpu as pltpu
from jax.sharding import PartitionSpec as P

TILE = 16
EXT = 16
LANES = 128
HIGHEST = lax.Precision.HIGHEST
BF = jnp.bfloat16
F32 = jnp.float32


def mxu(left, right):
    return jnp.dot(left, right, preferred_element_type=F32)


def block(x_ref, t_ref, offsets):
    rows = x_ref.shape[0]
    half = rows // 2
    depth = t_ref.shape[0]
    width = t_ref.shape[1] // 2
    windows = [x_ref[:, pl.ds(offset, depth)] for offset in offsets]
    result = mxu(jnp.concatenate(windows, axis=0), t_ref[...])
    result = result.reshape(len(offsets), rows, 2 * width)
    real = result[:, :half, :width] + result[:, half:, width:]
    imag = result[:, half:, :width] - result[:, :half, width:]
    return jnp.concatenate([real, imag], axis=1).astype(BF)


def butterfly(parts, sign):
    radix = len(parts)
    if radix == 1:
        return parts
    (ar, ai), (br, bi), (cr, ci), (dr, di) = parts
    pr, pi, qr, qi = ar + cr, ai + ci, ar - cr, ai - ci
    tr, ti, ur, ui = br + dr, bi + di, br - dr, bi - di
    return [
        (pr + tr, pi + ti),
        (qr - sign * ui, qi + sign * ur),
        (pr - tr, pi - ti),
        (qr + sign * ui, qi - sign * ur),
    ]


def forward(table_ref, subsets, length):
    parts = []
    for j, (yr, yi) in enumerate(subsets):
        c, s = table_ref[j, 0, :, :length], table_ref[j, 1, :, :length]
        parts.append((mxu(c, yr) + mxu(s, yi), mxu(c, yi) - mxu(s, yr)))
    return butterfly(parts, -1.0)


def replica_spectra(table_ref, g_ref, out_ref):
    radix, length = g_ref.shape[1], g_ref.shape[2]
    subsets = [(g_ref[0, j], g_ref[1, j]) for j in range(radix)]
    for m, pair in enumerate(forward(table_ref, subsets, length)):
        for part, value in enumerate(pair):
            high = value.astype(BF)
            low = (value - high.astype(F32)).astype(BF)
            out_ref[part, m] = jnp.concatenate([high, low], axis=1)


def azimuth(table_ref, back_ref, y_ref, g_ref, index, mask_ref, out_ref, sums_ref, blocks):
    devices, rows, width = y_ref.shape
    radix, _, quarter, _ = table_ref.shape
    piece = rows // (2 * radix)

    def store(ref, value):
        for i, number in enumerate(blocks):
            ref[:, number * LANES : (number + 1) * LANES] = value[:, i * LANES : (i + 1) * LANES]

    def subset(k):
        return y_ref[:, k * piece : (k + 1) * piece, :].reshape(quarter, width)

    spectrum = forward(table_ref, [(subset(j), subset(radix + j)) for j in range(radix)], quarter)
    replicas = g_ref.shape[3] // 2
    which = lax.rem(lax.broadcasted_iota(jnp.int32, (2 * replicas, width), 0), replicas)
    pick = (which == index).astype(BF)
    scale = 1.0 / (radix * quarter)
    product = []
    for m, (fr, fi) in enumerate(spectrum):
        gr = mxu(g_ref[0, m], pick) * scale
        gi = mxu(g_ref[1, m], pick) * scale
        product.append((fr * gr + fi * gi, fi * gr - fr * gi))
    sums = jnp.zeros((sums_ref.shape[0], width), F32)
    for j, (zr, zi) in enumerate(butterfly(product, 1.0)):
        zr, zi = zr.astype(BF), zi.astype(BF)
        c, s = back_ref[j, 0], back_ref[j, 1]
        ar = mxu(c, zr) - mxu(s, zi)
        ai = mxu(c, zi) + mxu(s, zr)
        store(out_ref.at[0, j], ar.astype(BF))
        store(out_ref.at[1, j], ai.astype(BF))
        power = ar * ar + ai * ai
        high = power.astype(BF)
        low = (power - high.astype(F32)).astype(BF)
        mask = mask_ref[j]
        sums = sums + mxu(mask, high) + mxu(mask, low)
    store(sums_ref, sums)


def focus_kernel(
    devices, bins, chunks,
    x_ref, taps_ref, g_ref, index_ref, mask_ref, table_hbm, back_hbm,
    out_ref, sums_ref, halo_ref,
    bands, packed, turned, table, back, spectra, edges, landed,
    send_sems, recv_sems, edge_send, edge_recv, table_sems,
):
    me = lax.axis_index("row")
    barrier = pltpu.get_barrier_semaphore()
    last = bins // LANES - 1
    loads = [
        pltpu.make_async_copy(table_hbm, table, table_sems.at[0]),
        pltpu.make_async_copy(back_hbm, back, table_sems.at[1]),
    ]
    for load in loads:
        load.start()

    def greet(i, carry):
        pl.semaphore_signal(
            barrier,
            inc=1,
            device_id={"row": lax.rem(me + i, devices)},
            device_id_type=pl.DeviceIdType.MESH,
        )
        return carry

    lax.fori_loop(1, devices, greet, 0)

    for part in range(2):
        taps = taps_ref[part : part + 1, :].astype(F32)
        taps = jnp.concatenate([taps, jnp.zeros((1, LANES), F32)], axis=1)
        taps = jnp.broadcast_to(taps, (LANES, taps.shape[1]))
        band = pltpu.roll(taps, 0, 1, stride=1, stride_axis=0)
        bands[:, part * LANES : (part + 1) * LANES] = band.T.astype(BF)

    def piece(q, target):
        offsets = [pl.multiple_of(target * bins + b * LANES, LANES) for b in chunks[q]]
        result = block(x_ref, bands, offsets)
        return jnp.concatenate([result[i] for i in range(len(offsets))], axis=1)

    def shift_of(t):
        return devices // 2 + (t + 1) // 2 * (1 - 2 * (t % 2))

    def remote(q, t):
        shift = shift_of(t)
        target = lax.rem(me + shift, devices)
        return pltpu.make_async_remote_copy(
            src_ref=packed.at[q, target],
            dst_ref=turned.at[q, me],
            send_sem=send_sems.at[q, shift],
            recv_sem=recv_sems.at[q, shift],
            device_id={"row": target},
            device_id_type=pl.DeviceIdType.MESH,
        )

    def edge(side):
        target = lax.rem(me + (devices - 1 if side == 0 else 1), devices)
        return pltpu.make_async_remote_copy(
            src_ref=edges.at[side],
            dst_ref=landed.at[1 - side],
            send_sem=edge_send.at[side],
            recv_sem=edge_recv.at[side],
            device_id={"row": target},
            device_id_type=pl.DeviceIdType.MESH,
        )

    for q in range(len(chunks)):
        def fill(t, carry, q=q):
            target = lax.rem(me + shift_of(t), devices)
            packed[q, target] = piece(q, target)
            if q > 0:
                remote(q, t).start()
            else:
                @pl.when(t == 0)
                def _():
                    pl.semaphore_wait(barrier, devices - 1)
                remote(q, t).start()
            return carry

        lax.fori_loop(0, devices - 1, fill, 0)
    for q in range(len(chunks)):
        turned[q, me] = piece(q, me)
    for load in loads:
        load.wait()
    replica_spectra(table, g_ref, spectra)

    for q, blocks in enumerate(chunks):
        def finish(t, carry, q=q):
            remote(q, t).wait()
            return carry

        lax.fori_loop(0, devices - 1, finish, 0)
        index = jnp.concatenate(
            [index_ref[:, b * LANES : (b + 1) * LANES] for b in blocks], axis=1
        )
        azimuth(
            table, back, turned.at[q], spectra, index, mask_ref, out_ref, sums_ref, blocks
        )
        for side, number in ((0, 0), (1, last)):
            if number in blocks:
                edges[side] = sums_ref[:, number * LANES : (number + 1) * LANES]
                edge(side).start()
    for side in (0, 1):
        edge(side).wait()
    halo_ref[...] = landed[...]


def focus(x, taps, g, index, mask, table, back, devices, bins):
    rows = x.shape[0]
    radix, _, quarter, _ = table.shape
    tiles = mask.shape[1]
    count = bins // LANES
    if count % 2:
        chunks = [(b,) for b in range(count)]
    else:
        chunks = [(b, count - 1 - b) for b in range(count // 2)]
    width = len(chunks[0]) * LANES
    vmem = pl.BlockSpec(memory_space=pltpu.VMEM)
    anywhere = pl.BlockSpec(memory_space=pl.ANY)
    pieces = pltpu.VMEM((len(chunks), devices, rows, width), BF)
    return pl.pallas_call(
        functools.partial(focus_kernel, devices, bins, chunks),
        in_specs=[vmem] * 5 + [anywhere] * 2,
        out_specs=(vmem, vmem, vmem),
        out_shape=(
            jax.ShapeDtypeStruct((2, radix, quarter, bins), BF),
            jax.ShapeDtypeStruct((tiles, bins), F32),
            jax.ShapeDtypeStruct((2, tiles, LANES), F32),
        ),
        scratch_shapes=[
            pltpu.VMEM((taps.shape[1] + LANES, 2 * LANES), BF),
            pieces,
            pieces,
            pltpu.VMEM(table.shape, BF),
            pltpu.VMEM(back.shape, BF),
            pltpu.VMEM((2, radix, quarter, 2 * g.shape[3]), BF),
            pltpu.VMEM((2, tiles, LANES), F32),
            pltpu.VMEM((2, tiles, LANES), F32),
            pltpu.SemaphoreType.DMA((len(chunks), devices)),
            pltpu.SemaphoreType.DMA((len(chunks), devices)),
            pltpu.SemaphoreType.DMA((2,)),
            pltpu.SemaphoreType.DMA((2,)),
            pltpu.SemaphoreType.DMA((2,)),
        ],
        compiler_params=pltpu.CompilerParams(
            collective_id=0, has_side_effects=True, vmem_limit_bytes=50 * 2**20
        ),
        name="focus",
    )(x, taps, g, index, mask, table, back)


def dft_tables(length, radix):
    quarter = length // radix
    freq = np.arange(quarter, dtype=np.int64)
    tables = []
    for j in range(radix):
        pulse = radix * np.arange(quarter, dtype=np.int64) + j
        angles = (np.outer(freq, pulse) % length) * (2.0 * np.pi / length)
        tables.append(np.stack([np.cos(angles), np.sin(angles)]))
    table = np.stack(tables)
    return jnp.asarray(table, dtype=BF), jnp.asarray(table.swapaxes(2, 3), dtype=BF)


def window_columns(positions, starts, stops):
    inside = (positions[:, None] >= starts[None, :]) & (positions[:, None] < stops[None, :])
    return inside.astype(F32)


def per_device(
    echoes, range_replica, azimuth_replicas, replica_index, azimuth_extent, range_extent
):
    devices = lax.axis_size("row")
    local_pulses, _, samples = echoes.shape
    taps = range_replica.shape[1]
    pulses = local_pulses * devices
    range_bins = samples // devices
    radix = 4 if local_pulses % 64 == 0 else 1
    quarter = pulses // radix

    rows = echoes.reshape(local_pulses // radix, radix, 2, samples).transpose(2, 1, 0, 3)
    rows = jnp.pad(rows.reshape(2 * local_pulses, samples), ((0, 0), (0, taps)))
    table, back = dft_tables(pulses, radix)
    replicas, _, azimuth_taps = azimuth_replicas.shape
    split = azimuth_replicas.reshape(replicas, 2, azimuth_taps // radix, radix)
    tile_rows = pulses // TILE
    pulse_start = jnp.arange(tile_rows, dtype=jnp.int32) * TILE - azimuth_extent
    pulse_stop = pulse_start + TILE + 2 * azimuth_extent
    order = jnp.arange(radix, dtype=jnp.int32)[:, None, None] + radix * jnp.arange(
        quarter, dtype=jnp.int32
    )
    pulse_mask = (order >= pulse_start[:, None]) & (order < pulse_stop[:, None])
    pulse_count = (jnp.minimum(pulse_stop, pulses) - jnp.maximum(pulse_start, 0)).astype(F32)
    pulse_mask = pulse_mask.astype(BF)

    index = replica_index.reshape(1, range_bins)
    image, sums, halo = focus(
        rows, range_replica, split.transpose(1, 3, 2, 0), index, pulse_mask, table, back,
        devices, range_bins,
    )
    focused = image.transpose(2, 1, 0, 3).reshape(pulses, 2, range_bins)
    before, after = halo[0, :, LANES - EXT :], halo[1, :, :EXT]
    row_sums = jnp.concatenate([before, sums, after], axis=1)

    local_tiles = range_bins // TILE
    device = lax.axis_index("row")
    tile_ids = device * local_tiles + jnp.arange(local_tiles, dtype=jnp.int32)
    local_extent = lax.dynamic_slice_in_dim(range_extent, device * local_tiles, local_tiles)
    range_start = tile_ids * TILE - local_extent
    range_stop = range_start + TILE + 2 * local_extent
    range_count = (
        jnp.minimum(range_stop, samples) - jnp.maximum(range_start, 0)
    ).astype(F32)
    positions = device * range_bins - EXT + jnp.arange(range_bins + 2 * EXT, dtype=jnp.int32)
    range_mask = window_columns(
        positions, jnp.maximum(range_start, 0), jnp.minimum(range_stop, samples)
    )
    window_sums = jnp.einsum(
        "ct,ic->ti", range_mask, row_sums, precision=HIGHEST, preferred_element_type=F32
    )
    looked = window_sums / (range_count[:, None] * pulse_count[None, :])
    return (focused, looked)


def solution(mesh):
    return jax.shard_map(
        per_device,
        mesh=mesh,
        in_specs=(
            P(("scene", "row"), None, None),
            P(),
            P(),
            P(("scene", "row")),
            P("scene"),
            P("scene"),
        ),
        out_specs=(P("scene", None, "row"), P(("scene", "row"), None)),
        check_vma=False,
    )
```

time: 87.4 us -> 70 us (0.80)
  waiting for transfers between devices: 46.4 us -> 0 us
  Pallas kernels: 16.3 us -> 56.7 us
  starting transfers between devices: 13.1 us -> 0 us
  local copies, waits for them, and re-layouts: 7.86 us -> 10.1 us
    all_to_all x1 -> x0, waiting for transfers between devices: 46.4 us -> none  [exchange(): lax.all_to_all(packed, 'row', split_axis=0, concat_axis=0, tiled=True)]
    pallas_call x4 -> x1, Pallas kernels: 16.3 us -> 56.7 us  [focus(): pl.pallas_call(functools.partial(focus_kernel, devices, bins, chunks), in...]
    all_to_all x1 -> x0, starting transfers between devices: 6.69 us -> none  [exchange(): lax.all_to_all(packed, 'row', split_axis=0, concat_axis=0, tiled=True)]
    ppermute x2 -> x0, starting transfers between devices: 6.45 us -> none  [the longest x1 4.34 us: per_device(): lax.ppermute(sums[:, range_bins - EXT:], 'row', [(i, i + 1) for i in rang...]
    transpose x1, local copies, waits for them, and re-layouts: 3.47 us -> 5.07 us  [per_device(): focused = image.transpose(2, 1, 0, 3).reshape(pulses, 2, range_bins)]
    pad x1, local copies, waits for them, and re-layouts: 0.2 us -> 1.62 us  [per_device(): rows = jnp.pad(rows.reshape(2 * local_pulses, samples), ((0, 0), (0, taps)))]
  transfers between devices with their start and end apart: 3 -> 0, of which waited for: 1 -> 0; matrix products, arithmetic and copies ran while one was open for 5% -> 0% of each run, Pallas kernels for 1% -> 0%
where the time goes in v3:
time: 70 us; the launch traced here: 69.5 us
  Pallas kernels  56.7 us (81%)
  local copies, waits for them, and re-layouts  10.1 us (14%)
  matrix products  1.08 us (2%)
  other arithmetic  0.89 us (1%)
  between operations  0.75 us (1%)
    pallas_call x1, Pallas kernels, focus(): pl.pallas_call(functools.partial(focus_kernel, devices, bins, chunks), in...  56.7 us
    transpose x1, local copies, waits for them, and re-layouts, per_device(): focused = image.transpose(2, 1, 0, 3).reshape(pulses, 2, range_bins)  5.07 us
    reshape x1, local copies, waits for them, and re-layouts, per_device(): echoes.reshape(local_pulses // radix, radix, 2, samples)  2.75 us
    pad x1, local copies, waits for them, and re-layouts, per_device(): rows = jnp.pad(rows.reshape(2 * local_pulses, samples), ((0, 0), (0, taps)))  1.62 us

profile of v3, /device:TPU:15, one launch (start us, length us, event | category | flops | bytes accessed | tf_op | source)
XLA Modules:
  0.0 69.5 jit_solution(6567989103535792674)
XLA Ops:
  0.6 2.8 %copy.11 = bf16[16,4,2,8192]{3,0,1,2:T(8,128)(2,1)S(1)} copy(bf16[16,4,2,8192]{3,2,1,0:T(2,128)(2,1)} %bitcast.18) | data formatting | bytes 4194304 | tf_op jit(solution)/shard_map/reshape | solution.py:286
  3.4 0.0 copy-start.4
  3.4 0.0 copy-start.5
  3.4 0.0 copy-start
  3.4 0.0 copy-start.1
  3.4 0.0 copy-start.2
  3.4 0.0 copy-start.3
  3.5 1.6 %pad.4.x_ref = bf16[128,9216]{1,0:T(8,128)(2,1)} pad(bf16[128,8192]{1,0:T(8,128)(2,1)S(1)} %bitcast.17, bf16[]{:T(256)} %constant.13.clone.1), padding=0_0x0_1024 | pad | bytes 4456450 | tf_op jit(solution)/shard_map/jit(_pad)/pad | solution.py:287
  5.1 0.0 copy-done.4
  5.1 0.2 copy.12
  5.3 0.0 copy-done.5
  5.4 0.1 and_convert_fusion.1.mask_ref
  5.5 0.0 copy-done
  5.5 0.3 copy-done.1
  5.8 0.0 copy-done.2
  5.8 0.0 copy-done.3
  5.8 56.7 %focus.1 = (bf16[2,4,256,512]{3,2,1,0:T(8,128)(2,1)}, f32[64,512]{1,0:T(8,128)S(1)}, f32[2,64,128]{2,1,0:T(8,128)S(1)}) custom-call(bf16[128,9216]{1,0:T(8,128)(2,1)} %pad.4.x_ref, bf16[2,1024]{1,0:T(2,128)(2,1)S(1)} %copy-done.2, bf16[2,4,128,16]{3,2,1,0:T(8,128)(2,1)S(1)} %bitcast.15, s32[1,512]{1,0:T(1,128)S(1)} %bitcast.16, ...), custom_call_target="tpu_custom_call" | custom-call | tf_op jit(solution)/shard_map/focus/pallas_call | solution.py:227
  62.5 5.1 %copy.14 = bf16[256,4,2,512]{3,2,1,0:T(2,128)(2,1)} copy(bf16[256,4,2,512]{3,0,1,2:T(8,128)(2,1)} %bitcast.20) | data formatting | bytes 4194304 | tf_op jit(solution)/shard_map/transpose | solution.py:306
  67.6 0.1 slice_bitcast_fusion.1
  67.6 0.8 %subtract_convert_fusion.1 = (f32[32]{0:T(128)S(1)}, s32[32]{0:T(128)S(1)}, s32[32]{0:T(128)S(1)}) fusion(s32[512]{0:T(512)} %param.13, s32[]{:T(128)S(6)} %select_n.3, s32[]{:T(128)S(6)} %mul.56), kind=kLoop, calls=%fused_computation.18 | loop fusion | flops 320 | bytes 520 | tf_op jit(solution)/shard_map/convert_element_type | solution.py:318
  68.4 1.1 %convolution_divide_fusion = f32[32,64]{1,0:T(8,128)} fusion(f32[64,16]{1,0:T(8,128)S(1)} %get-tuple-element.12, f32[64,512]{1,0:T(8,128)S(1)} %get-tuple-element.7, f32[64,16]{1,0:T(8,128)S(1)} %get-tuple-element.11, s32[32]{0:T(128)S(1)} %get-tuple-element.9, s32[32]{0:T(128)S(1)} %broadcast_maximum_fusion, s32[544]{0:T(1024)S(1)} %iota_add_fusion, ...), kind=kOutput, calls=%fused_computation | convolution fusion | flops 13512704 | bytes 150272 | tf_op jit(solution)/shard_map/ct,ic->ti/dot_general | solution.py:323
  (6 shorter events, 0.1 us)
Async XLA Ops:
  3.4 1.7 %copy-start.4 = (bf16[16,2,512]{2,1,0:T(2,128)(2,1)S(1)}, bf16[16,2,512]{2,1,0:T(2,128)(2,1)}, u32[]{:S(2)}) copy-start(bf16[16,2,512]{2,1,0:T(2,128)(2,1)} %param.10) | copy-start | bytes 98308
  3.4 1.9 %copy-start.5 = (s32[64]{0:T(128)S(1)}, s32[64]{0:T(128)}, u32[]{:S(2)}) copy-start(s32[64]{0:T(128)} %param.12) | copy-start | bytes 772
  3.4 2.1 %copy-start = (bf16[4,2,256,256]{3,2,1,0:T(8,128)(2,1)S(1)}, bf16[4,2,256,256]{3,2,1,0:T(8,128)(2,1)}, u32[]{:S(2)}) copy-start(bf16[4,2,256,256]{3,2,1,0:T(8,128)(2,1)} %constant.12.clone.table_hbm) | copy-start | bytes 3145732
  3.4 2.4 %copy-start.1 = (bf16[4,2,256,256]{3,2,1,0:T(8,128)(2,1)S(1)}, bf16[4,2,256,256]{3,2,1,0:T(8,128)(2,1)}, u32[]{:S(2)}) copy-start(bf16[4,2,256,256]{3,2,1,0:T(8,128)(2,1)} %constant.34.clone.back_hbm) | copy-start | bytes 3145732
  3.4 2.4 %copy-start.2 = (bf16[2,1024]{1,0:T(2,128)(2,1)S(1)}, bf16[2,1024]{1,0:T(2,128)(2,1)}, u32[]{:S(2)}) copy-start(bf16[2,1024]{1,0:T(2,128)(2,1)} %taps_ref.1) | copy-start | bytes 12292
  3.4 2.4 %copy-start.3 = (s32[512]{0:T(512)S(1)}, s32[512]{0:T(512)}, u32[]{:S(2)}) copy-start(s32[512]{0:T(512)} %param.11) | copy-start | bytes 6148

commit v4 on v3

--- a/solution.py
+++ b/solution.py
@@ -106,9 +106,9 @@
 
 def focus_kernel(
     devices, bins, chunks,
-    x_ref, taps_ref, g_ref, index_ref, mask_ref, table_hbm, back_hbm,
+    x_hbm, taps_ref, g_ref, index_ref, mask_ref, table_hbm, back_hbm,
     out_ref, sums_ref, halo_ref,
-    bands, packed, turned, table, back, spectra, edges, landed,
+    x_ref, bands, packed, turned, table, back, spectra, edges, landed,
     send_sems, recv_sems, edge_send, edge_recv, table_sems,
 ):
     me = lax.axis_index("row")
@@ -118,8 +118,12 @@
         pltpu.make_async_copy(table_hbm, table, table_sems.at[0]),
         pltpu.make_async_copy(back_hbm, back, table_sems.at[1]),
     ]
+    samples = x_hbm.shape[1]
+    echoes = pltpu.make_async_copy(x_hbm, x_ref.at[:, :samples], table_sems.at[2])
+    echoes.start()
     for load in loads:
         load.start()
+    x_ref[:, samples:] = jnp.zeros((x_ref.shape[0], x_ref.shape[1] - samples), BF)
 
     def greet(i, carry):
         pl.semaphore_signal(
@@ -138,6 +142,8 @@
         taps = jnp.broadcast_to(taps, (LANES, taps.shape[1]))
         band = pltpu.roll(taps, 0, 1, stride=1, stride_axis=0)
         bands[:, part * LANES : (part + 1) * LANES] = band.T.astype(BF)
+
+    echoes.wait()
 
     def piece(q, target):
         offsets = [pl.multiple_of(target * bins + b * LANES, LANES) for b in chunks[q]]
@@ -226,7 +232,7 @@
     pieces = pltpu.VMEM((len(chunks), devices, rows, width), BF)
     return pl.pallas_call(
         functools.partial(focus_kernel, devices, bins, chunks),
-        in_specs=[vmem] * 5 + [anywhere] * 2,
+        in_specs=[anywhere] + [vmem] * 4 + [anywhere] * 2,
         out_specs=(vmem, vmem, vmem),
         out_shape=(
             jax.ShapeDtypeStruct((2, radix, quarter, bins), BF),
@@ -234,6 +240,7 @@
             jax.ShapeDtypeStruct((2, tiles, LANES), F32),
         ),
         scratch_shapes=[
+            pltpu.VMEM((rows, x.shape[1] + taps.shape[1]), BF),
             pltpu.VMEM((taps.shape[1] + LANES, 2 * LANES), BF),
             pieces,
             pieces,
@@ -246,10 +253,10 @@
             pltpu.SemaphoreType.DMA((len(chunks), devices)),
             pltpu.SemaphoreType.DMA((2,)),
             pltpu.SemaphoreType.DMA((2,)),
-            pltpu.SemaphoreType.DMA((2,)),
+            pltpu.SemaphoreType.DMA((3,)),
         ],
         compiler_params=pltpu.CompilerParams(
-            collective_id=0, has_side_effects=True, vmem_limit_bytes=50 * 2**20
+            collective_id=0, has_side_effects=True, vmem_limit_bytes=28 * 2**20
         ),
         name="focus",
     )(x, taps, g, index, mask, table, back)
@@ -277,14 +284,13 @@
 ):
     devices = lax.axis_size("row")
     local_pulses, _, samples = echoes.shape
-    taps = range_replica.shape[1]
     pulses = local_pulses * devices
     range_bins = samples // devices
     radix = 4 if local_pulses % 64 == 0 else 1
     quarter = pulses // radix
 
     rows = echoes.reshape(local_pulses // radix, radix, 2, samples).transpose(2, 1, 0, 3)
-    rows = jnp.pad(rows.reshape(2 * local_pulses, samples), ((0, 0), (0, taps)))
+    rows = rows.reshape(2 * local_pulses, samples)
     table, back = dft_tables(pulses, radix)
     replicas, _, azimuth_taps = azimuth_replicas.shape
     split = azimuth_replicas.reshape(replicas, 2, azimuth_taps // radix, radix)

time: 70 us -> 64.9 us (0.927)
  Pallas kernels: 56.7 us -> 53.9 us
  local copies, waits for them, and re-layouts: 10.1 us -> 7.85 us
    pallas_call x1, Pallas kernels: 56.7 us -> 53.9 us  [focus(): pl.pallas_call(functools.partial(focus_kernel, devices, bins, chunks), in...]
    pad x1 -> x0, local copies, waits for them, and re-layouts: 1.62 us -> none  [per_device(): rows = jnp.pad(rows.reshape(2 * local_pulses, samples), ((0, 0), (0, taps)))]
    transpose x1, local copies, waits for them, and re-layouts: 5.07 us -> 3.48 us  [per_device(): focused = image.transpose(2, 1, 0, 3).reshape(pulses, 2, range_bins)]
    unnamed x13, local copies, waits for them, and re-layouts: 0.55 us -> 1.43 us
where the time goes in v4:
time: 64.9 us; the launch traced here: 64.5 us
  Pallas kernels  53.9 us (83%)
  local copies, waits for them, and re-layouts  7.85 us (12%)
  matrix products  1.08 us (2%)
  other arithmetic  0.89 us (1%)
  between operations  0.78 us (1%)
    pallas_call x1, Pallas kernels, focus(): pl.pallas_call(functools.partial(focus_kernel, devices, bins, chunks), in...  53.9 us
    transpose x1, local copies, waits for them, and re-layouts, per_device(): focused = image.transpose(2, 1, 0, 3).reshape(pulses, 2, range_bins)  3.48 us
    reshape x1, local copies, waits for them, and re-layouts, per_device(): echoes.reshape(local_pulses // radix, radix, 2, samples)  2.84 us
    unnamed x13, local copies, waits for them, and re-layouts  1.43 us

profile of v4, /device:TPU:15, one launch (start us, length us, event | category | flops | bytes accessed | tf_op | source)
XLA Modules:
  0.0 64.5 jit_solution(5997376710990376511)
XLA Ops:
  0.6 0.0 copy-start.4
  0.6 0.0 copy-start.5
  0.7 0.0 copy-start
  0.7 0.0 copy-start.2
  0.7 0.0 copy-start.3
  0.7 2.8 %copy.11 = bf16[16,4,2,8192]{3,0,1,2:T(8,128)(2,1)S(1)} copy(bf16[16,4,2,8192]{3,2,1,0:T(2,128)(2,1)} %bitcast.19) | data formatting | bytes 4194304 | tf_op jit(solution)/shard_map/reshape | solution.py:292
  3.5 0.0 copy-done.4
  3.5 0.2 copy.12
  3.8 0.0 copy-done.5
  3.8 0.1 and_convert_fusion.1.mask_ref
  3.9 0.0 copy-done
  3.9 0.0 copy-done.2
  4.0 0.0 copy-done.3
  4.0 0.0 copy-start.1
  4.0 1.2 %copy-done.1 = bf16[4,2,256,256]{3,2,1,0:T(8,128)(2,1)S(1)} copy-done((bf16[4,2,256,256]{3,2,1,0:T(8,128)(2,1)S(1)}, bf16[4,2,256,256]{3,2,1,0:T(8,128)(2,1)}, u32[]{:S(2)}) %copy-start.1) | copy-done | bytes 1048600
  5.2 53.9 %focus.1 = (bf16[2,4,256,512]{3,2,1,0:T(8,128)(2,1)S(1)}, f32[64,512]{1,0:T(8,128)S(1)}, f32[2,64,128]{2,1,0:T(8,128)S(1)}) custom-call(bf16[128,8192]{1,0:T(8,128)(2,1)S(1)} %bitcast.15, bf16[2,1024]{1,0:T(2,128)(2,1)S(1)} %copy-done.2, bf16[2,4,128,16]{3,2,1,0:T(8,128)(2,1)S(1)} %bitcast.17, s32[1,512]{1,0:T(1,128)S(1)} %bitcast.18, ...), custom_call_target="tpu_custom_call" | custom-call | tf_op jit(solution)/shard_map/focus/pallas_call | solution.py:233
  59.1 3.5 %copy.14 = bf16[256,4,2,512]{3,2,1,0:T(2,128)(2,1)} copy(bf16[256,4,2,512]{3,0,1,2:T(8,128)(2,1)S(1)} %bitcast.16) | data formatting | bytes 4194304 | tf_op jit(solution)/shard_map/transpose | solution.py:312
  62.5 0.1 slice_bitcast_fusion.1
  62.6 0.8 %subtract_convert_fusion.1 = (f32[32]{0:T(128)S(1)}, s32[32]{0:T(128)S(1)}, s32[32]{0:T(128)S(1)}) fusion(s32[512]{0:T(512)} %param.13, s32[]{:T(128)S(6)} %select_n.3, s32[]{:T(128)S(6)} %mul.56), kind=kLoop, calls=%fused_computation.18 | loop fusion | flops 320 | bytes 520 | tf_op jit(solution)/shard_map/convert_element_type | solution.py:324
  63.4 1.1 %convolution_divide_fusion = f32[32,64]{1,0:T(8,128)} fusion(f32[64,16]{1,0:T(8,128)S(1)} %get-tuple-element.12, f32[64,512]{1,0:T(8,128)S(1)} %get-tuple-element.7, f32[64,16]{1,0:T(8,128)S(1)} %get-tuple-element.11, s32[32]{0:T(128)S(1)} %get-tuple-element.9, s32[32]{0:T(128)S(1)} %broadcast_maximum_fusion, s32[544]{0:T(1024)S(1)} %iota_add_fusion, ...), kind=kOutput, calls=%fused_computation | convolution fusion | flops 13512704 | bytes 150272 | tf_op jit(solution)/shard_map/ct,ic->ti/dot_general | solution.py:329
  (6 shorter events, 0.1 us)
Async XLA Ops:
  0.6 2.9 %copy-start.4 = (bf16[16,2,512]{2,1,0:T(2,128)(2,1)S(1)}, bf16[16,2,512]{2,1,0:T(2,128)(2,1)}, u32[]{:S(2)}) copy-start(bf16[16,2,512]{2,1,0:T(2,128)(2,1)} %param.10) | copy-start | bytes 98308
  0.6 3.2 %copy-start.5 = (s32[64]{0:T(128)S(1)}, s32[64]{0:T(128)}, u32[]{:S(2)}) copy-start(s32[64]{0:T(128)} %param.12) | copy-start | bytes 772
  0.7 3.3 %copy-start = (bf16[4,2,256,256]{3,2,1,0:T(8,128)(2,1)S(1)}, bf16[4,2,256,256]{3,2,1,0:T(8,128)(2,1)}, u32[]{:S(2)}) copy-start(bf16[4,2,256,256]{3,2,1,0:T(8,128)(2,1)} %constant.9.clone.table_hbm) | copy-start | bytes 3145732
  0.7 3.3 %copy-start.2 = (bf16[2,1024]{1,0:T(2,128)(2,1)S(1)}, bf16[2,1024]{1,0:T(2,128)(2,1)}, u32[]{:S(2)}) copy-start(bf16[2,1024]{1,0:T(2,128)(2,1)} %taps_ref.1) | copy-start | bytes 12292
  0.7 3.3 %copy-start.3 = (s32[512]{0:T(512)S(1)}, s32[512]{0:T(512)}, u32[]{:S(2)}) copy-start(s32[512]{0:T(512)} %param.11) | copy-start | bytes 6148
  4.0 1.2 %copy-start.1 = (bf16[4,2,256,256]{3,2,1,0:T(8,128)(2,1)S(1)}, bf16[4,2,256,256]{3,2,1,0:T(8,128)(2,1)}, u32[]{:S(2)}) copy-start(bf16[4,2,256,256]{3,2,1,0:T(8,128)(2,1)} %constant.10.clone.back_hbm) | copy-start | bytes 3145732

commit v5 on v4

--- a/solution.py
+++ b/solution.py
@@ -106,7 +106,7 @@
 
 def focus_kernel(
     devices, bins, chunks,
-    x_hbm, taps_ref, g_ref, index_ref, mask_ref, table_hbm, back_hbm,
+    x_hbm, taps_ref, g_ref, index_ref, mask_ref, table_hbm,
     out_ref, sums_ref, halo_ref,
     x_ref, bands, packed, turned, table, back, spectra, edges, landed,
     send_sems, recv_sems, edge_send, edge_recv, table_sems,
@@ -114,15 +114,11 @@
     me = lax.axis_index("row")
     barrier = pltpu.get_barrier_semaphore()
     last = bins // LANES - 1
-    loads = [
-        pltpu.make_async_copy(table_hbm, table, table_sems.at[0]),
-        pltpu.make_async_copy(back_hbm, back, table_sems.at[1]),
-    ]
+    load = pltpu.make_async_copy(table_hbm, table, table_sems.at[0])
     samples = x_hbm.shape[1]
-    echoes = pltpu.make_async_copy(x_hbm, x_ref.at[:, :samples], table_sems.at[2])
+    echoes = pltpu.make_async_copy(x_hbm, x_ref.at[:, :samples], table_sems.at[1])
     echoes.start()
-    for load in loads:
-        load.start()
+    load.start()
     x_ref[:, samples:] = jnp.zeros((x_ref.shape[0], x_ref.shape[1] - samples), BF)
 
     def greet(i, carry):
@@ -192,8 +188,10 @@
         lax.fori_loop(0, devices - 1, fill, 0)
     for q in range(len(chunks)):
         turned[q, me] = piece(q, me)
-    for load in loads:
-        load.wait()
+    load.wait()
+    for j in range(table.shape[0]):
+        for part in range(2):
+            back[j, part] = table[j, part].astype(F32).T.astype(BF)
     replica_spectra(table, g_ref, spectra)
 
     for q, blocks in enumerate(chunks):
@@ -217,7 +215,7 @@
     halo_ref[...] = landed[...]
 
 
-def focus(x, taps, g, index, mask, table, back, devices, bins):
+def focus(x, taps, g, index, mask, table, devices, bins):
     rows = x.shape[0]
     radix, _, quarter, _ = table.shape
     tiles = mask.shape[1]
@@ -232,7 +230,7 @@
     pieces = pltpu.VMEM((len(chunks), devices, rows, width), BF)
     return pl.pallas_call(
         functools.partial(focus_kernel, devices, bins, chunks),
-        in_specs=[anywhere] + [vmem] * 4 + [anywhere] * 2,
+        in_specs=[anywhere] + [vmem] * 4 + [anywhere],
         out_specs=(vmem, vmem, vmem),
         out_shape=(
             jax.ShapeDtypeStruct((2, radix, quarter, bins), BF),
@@ -245,7 +243,7 @@
             pieces,
             pieces,
             pltpu.VMEM(table.shape, BF),
-            pltpu.VMEM(back.shape, BF),
+            pltpu.VMEM(table.shape, BF),
             pltpu.VMEM((2, radix, quarter, 2 * g.shape[3]), BF),
             pltpu.VMEM((2, tiles, LANES), F32),
             pltpu.VMEM((2, tiles, LANES), F32),
@@ -253,13 +251,13 @@
             pltpu.SemaphoreType.DMA((len(chunks), devices)),
             pltpu.SemaphoreType.DMA((2,)),
             pltpu.SemaphoreType.DMA((2,)),
-            pltpu.SemaphoreType.DMA((3,)),
+            pltpu.SemaphoreType.DMA((2,)),
         ],
         compiler_params=pltpu.CompilerParams(
             collective_id=0, has_side_effects=True, vmem_limit_bytes=28 * 2**20
         ),
         name="focus",
-    )(x, taps, g, index, mask, table, back)
+    )(x, taps, g, index, mask, table)
 
 
 def dft_tables(length, radix):
@@ -271,7 +269,7 @@
         angles = (np.outer(freq, pulse) % length) * (2.0 * np.pi / length)
         tables.append(np.stack([np.cos(angles), np.sin(angles)]))
     table = np.stack(tables)
-    return jnp.asarray(table, dtype=BF), jnp.asarray(table.swapaxes(2, 3), dtype=BF)
+    return jnp.asarray(table, dtype=BF)
 
 
 def window_columns(positions, starts, stops):
@@ -291,7 +289,7 @@
 
     rows = echoes.reshape(local_pulses // radix, radix, 2, samples).transpose(2, 1, 0, 3)
     rows = rows.reshape(2 * local_pulses, samples)
-    table, back = dft_tables(pulses, radix)
+    table = dft_tables(pulses, radix)
     replicas, _, azimuth_taps = azimuth_replicas.shape
     split = azimuth_replicas.reshape(replicas, 2, azimuth_taps // radix, radix)
     tile_rows = pulses // TILE
@@ -306,7 +304,7 @@
 
     index = replica_index.reshape(1, range_bins)
     image, sums, halo = focus(
-        rows, range_replica, split.transpose(1, 3, 2, 0), index, pulse_mask, table, back,
+        rows, range_replica, split.transpose(1, 3, 2, 0), index, pulse_mask, table,
         devices, range_bins,
     )
     focused = image.transpose(2, 1, 0, 3).reshape(pulses, 2, range_bins)

time: 64.9 us -> 63.6 us (0.980)
  local copies, waits for them, and re-layouts: 7.85 us -> 6.63 us
    unnamed x13 -> x11, local copies, waits for them, and re-layouts: 1.43 us -> 0.21 us
where the time goes in v5:
time: 63.6 us; the launch traced here: 63.2 us
  Pallas kernels  53.8 us (85%)
  local copies, waits for them, and re-layouts  6.63 us (10%)
  matrix products  1.08 us (2%)
  other arithmetic  0.89 us (1%)
  between operations  0.77 us (1%)
    pallas_call x1, Pallas kernels, focus(): pl.pallas_call(functools.partial(focus_kernel, devices, bins, chunks), in...  53.8 us
    transpose x1, local copies, waits for them, and re-layouts, per_device(): focused = image.transpose(2, 1, 0, 3).reshape(pulses, 2, range_bins)  3.48 us
    reshape x1, local copies, waits for them, and re-layouts, per_device(): echoes.reshape(local_pulses // radix, radix, 2, samples)  2.84 us

profile of v5, /device:TPU:15, one launch (start us, length us, event | category | flops | bytes accessed | tf_op | source)
XLA Modules:
  0.0 63.2 jit_solution(4295223569635088149)
XLA Ops:
  0.6 0.0 copy-start.3
  0.6 0.0 copy-start.4
  0.7 0.0 copy-start
  0.7 0.0 copy-start.1
  0.7 0.0 copy-start.2
  0.7 2.8 %copy.10 = bf16[16,4,2,8192]{3,0,1,2:T(8,128)(2,1)S(1)} copy(bf16[16,4,2,8192]{3,2,1,0:T(2,128)(2,1)} %bitcast.19) | data formatting | bytes 4194304 | tf_op jit(solution)/shard_map/reshape | solution.py:290
  3.5 0.0 copy-done.3
  3.5 0.2 copy.11
  3.8 0.0 copy-done.4
  3.8 0.1 and_convert_fusion.1.mask_ref
  3.9 0.0 copy-done
  3.9 0.0 copy-done.1
  4.0 0.0 copy-done.2
  4.0 53.8 %focus.1 = (bf16[2,4,256,512]{3,2,1,0:T(8,128)(2,1)S(1)}, f32[64,512]{1,0:T(8,128)S(1)}, f32[2,64,128]{2,1,0:T(8,128)S(1)}) custom-call(bf16[128,8192]{1,0:T(8,128)(2,1)S(1)} %bitcast.15, bf16[2,1024]{1,0:T(2,128)(2,1)S(1)} %copy-done.1, bf16[2,4,128,16]{3,2,1,0:T(8,128)(2,1)S(1)} %bitcast.17, s32[1,512]{1,0:T(1,128)S(1)} %bitcast.18, ...), custom_call_target="tpu_custom_call" | custom-call | tf_op jit(solution)/shard_map/focus/pallas_call | solution.py:231
  57.8 3.5 %copy.13 = bf16[256,4,2,512]{3,2,1,0:T(2,128)(2,1)} copy(bf16[256,4,2,512]{3,0,1,2:T(8,128)(2,1)S(1)} %bitcast.16) | data formatting | bytes 4194304 | tf_op jit(solution)/shard_map/transpose | solution.py:310
  61.3 0.1 slice_bitcast_fusion.1
  61.3 0.8 %subtract_convert_fusion.1 = (f32[32]{0:T(128)S(1)}, s32[32]{0:T(128)S(1)}, s32[32]{0:T(128)S(1)}) fusion(s32[512]{0:T(512)} %param.12, s32[]{:T(128)S(6)} %select_n.3, s32[]{:T(128)S(6)} %mul.56), kind=kLoop, calls=%fused_computation.18 | loop fusion | flops 320 | bytes 520 | tf_op jit(solution)/shard_map/convert_element_type | solution.py:322
  62.1 1.1 %convolution_divide_fusion = f32[32,64]{1,0:T(8,128)} fusion(f32[64,16]{1,0:T(8,128)S(1)} %get-tuple-element.12, f32[64,512]{1,0:T(8,128)S(1)} %get-tuple-element.7, f32[64,16]{1,0:T(8,128)S(1)} %get-tuple-element.11, s32[32]{0:T(128)S(1)} %get-tuple-element.9, s32[32]{0:T(128)S(1)} %broadcast_maximum_fusion, s32[544]{0:T(1024)S(1)} %iota_add_fusion, ...), kind=kOutput, calls=%fused_computation | convolution fusion | flops 13512704 | bytes 150272 | tf_op jit(solution)/shard_map/ct,ic->ti/dot_general | solution.py:327
  (6 shorter events, 0.1 us)
Async XLA Ops:
  0.6 2.9 %copy-start.3 = (bf16[16,2,512]{2,1,0:T(2,128)(2,1)S(1)}, bf16[16,2,512]{2,1,0:T(2,128)(2,1)}, u32[]{:S(2)}) copy-start(bf16[16,2,512]{2,1,0:T(2,128)(2,1)} %param.9) | copy-start | bytes 98308
  0.6 3.2 %copy-start.4 = (s32[64]{0:T(128)S(1)}, s32[64]{0:T(128)}, u32[]{:S(2)}) copy-start(s32[64]{0:T(128)} %param.11) | copy-start | bytes 772
  0.7 3.3 %copy-start = (bf16[4,2,256,256]{3,2,1,0:T(8,128)(2,1)S(1)}, bf16[4,2,256,256]{3,2,1,0:T(8,128)(2,1)}, u32[]{:S(2)}) copy-start(bf16[4,2,256,256]{3,2,1,0:T(8,128)(2,1)} %constant.8.clone.table_hbm) | copy-start | bytes 3145732
  0.7 3.3 %copy-start.1 = (bf16[2,1024]{1,0:T(2,128)(2,1)S(1)}, bf16[2,1024]{1,0:T(2,128)(2,1)}, u32[]{:S(2)}) copy-start(bf16[2,1024]{1,0:T(2,128)(2,1)} %taps_ref.1) | copy-start | bytes 12292
  0.7 3.3 %copy-start.2 = (s32[512]{0:T(512)S(1)}, s32[512]{0:T(512)}, u32[]{:S(2)}) copy-start(s32[512]{0:T(512)} %param.10) | copy-start | bytes 6148

commit v6 on v5

--- a/solution.py
+++ b/solution.py
@@ -220,10 +220,7 @@
     radix, _, quarter, _ = table.shape
     tiles = mask.shape[1]
     count = bins // LANES
-    if count % 2:
-        chunks = [(b,) for b in range(count)]
-    else:
-        chunks = [(b, count - 1 - b) for b in range(count // 2)]
+    chunks = [(b,) for b in sorted(range(count), key=lambda b: min(b, count - 1 - b))]
     width = len(chunks[0]) * LANES
     vmem = pl.BlockSpec(memory_space=pltpu.VMEM)
     anywhere = pl.BlockSpec(memory_space=pl.ANY)

time: 63.6 us -> 64.9 us (1.020)
  the two profiles are of different devices: /device:TPU:15 before, /device:TPU:0 now
where the time goes in v6:
time: 64.9 us; the launch traced here: 64.8 us
  Pallas kernels  55.4 us (85%)
  local copies, waits for them, and re-layouts  6.63 us (10%)
  matrix products  1.08 us (2%)
  other arithmetic  0.89 us (1%)
  between operations  0.77 us (1%)
    pallas_call x1, Pallas kernels, focus(): pl.pallas_call(functools.partial(focus_kernel, devices, bins, chunks), in...  55.4 us
    transpose x1, local copies, waits for them, and re-layouts, per_device(): focused = image.transpose(2, 1, 0, 3).reshape(pulses, 2, range_bins)  3.48 us
    reshape x1, local copies, waits for them, and re-layouts, per_device(): echoes.reshape(local_pulses // radix, radix, 2, samples)  2.84 us

profile of v6, /device:TPU:0, one launch (start us, length us, event | category | flops | bytes accessed | tf_op | source)
XLA Modules:
  0.0 64.8 jit_solution(1687797148098696804)
XLA Ops:
  0.6 0.0 copy-start.3
  0.6 0.0 copy-start.4
  0.7 0.0 copy-start
  0.7 0.0 copy-start.1
  0.7 0.0 copy-start.2
  0.7 2.8 %copy.10 = bf16[16,4,2,8192]{3,0,1,2:T(8,128)(2,1)S(1)} copy(bf16[16,4,2,8192]{3,2,1,0:T(2,128)(2,1)} %bitcast.19) | data formatting | bytes 4194304 | tf_op jit(solution)/shard_map/reshape | solution.py:287
  3.5 0.0 copy-done.3
  3.5 0.2 copy.11
  3.8 0.0 copy-done.4
  3.8 0.1 and_convert_fusion.1.mask_ref
  3.9 0.0 copy-done
  3.9 0.0 copy-done.1
  4.0 0.0 copy-done.2
  4.0 55.4 %focus.1 = (bf16[2,4,256,512]{3,2,1,0:T(8,128)(2,1)S(1)}, f32[64,512]{1,0:T(8,128)S(1)}, f32[2,64,128]{2,1,0:T(8,128)S(1)}) custom-call(bf16[128,8192]{1,0:T(8,128)(2,1)S(1)} %bitcast.15, bf16[2,1024]{1,0:T(2,128)(2,1)S(1)} %copy-done.1, bf16[2,4,128,16]{3,2,1,0:T(8,128)(2,1)S(1)} %bitcast.17, s32[1,512]{1,0:T(1,128)S(1)} %bitcast.18, ...), custom_call_target="tpu_custom_call" | custom-call | tf_op jit(solution)/shard_map/focus/pallas_call | solution.py:228
  59.4 3.5 %copy.13 = bf16[256,4,2,512]{3,2,1,0:T(2,128)(2,1)} copy(bf16[256,4,2,512]{3,0,1,2:T(8,128)(2,1)S(1)} %bitcast.16) | data formatting | bytes 4194304 | tf_op jit(solution)/shard_map/transpose | solution.py:307
  62.8 0.1 slice_bitcast_fusion.1
  62.9 0.8 %subtract_convert_fusion.1 = (f32[32]{0:T(128)S(1)}, s32[32]{0:T(128)S(1)}, s32[32]{0:T(128)S(1)}) fusion(s32[512]{0:T(512)} %param.12, s32[]{:T(128)S(6)} %select_n.3, s32[]{:T(128)S(6)} %mul.56), kind=kLoop, calls=%fused_computation.18 | loop fusion | flops 320 | bytes 520 | tf_op jit(solution)/shard_map/convert_element_type | solution.py:319
  63.7 1.1 %convolution_divide_fusion = f32[32,64]{1,0:T(8,128)} fusion(f32[64,16]{1,0:T(8,128)S(1)} %get-tuple-element.12, f32[64,512]{1,0:T(8,128)S(1)} %get-tuple-element.7, f32[64,16]{1,0:T(8,128)S(1)} %get-tuple-element.11, s32[32]{0:T(128)S(1)} %get-tuple-element.9, s32[32]{0:T(128)S(1)} %broadcast_maximum_fusion, s32[544]{0:T(1024)S(1)} %iota_add_fusion, ...), kind=kOutput, calls=%fused_computation | convolution fusion | flops 13512704 | bytes 150272 | tf_op jit(solution)/shard_map/ct,ic->ti/dot_general | solution.py:324
  (6 shorter events, 0.1 us)
Async XLA Ops:
  0.6 2.9 %copy-start.3 = (bf16[16,2,512]{2,1,0:T(2,128)(2,1)S(1)}, bf16[16,2,512]{2,1,0:T(2,128)(2,1)}, u32[]{:S(2)}) copy-start(bf16[16,2,512]{2,1,0:T(2,128)(2,1)} %param.9) | copy-start | bytes 98308
  0.6 3.2 %copy-start.4 = (s32[64]{0:T(128)S(1)}, s32[64]{0:T(128)}, u32[]{:S(2)}) copy-start(s32[64]{0:T(128)} %param.11) | copy-start | bytes 772
  0.7 3.3 %copy-start = (bf16[4,2,256,256]{3,2,1,0:T(8,128)(2,1)S(1)}, bf16[4,2,256,256]{3,2,1,0:T(8,128)(2,1)}, u32[]{:S(2)}) copy-start(bf16[4,2,256,256]{3,2,1,0:T(8,128)(2,1)} %constant.8.clone.table_hbm) | copy-start | bytes 3145732
  0.7 3.3 %copy-start.1 = (bf16[2,1024]{1,0:T(2,128)(2,1)S(1)}, bf16[2,1024]{1,0:T(2,128)(2,1)}, u32[]{:S(2)}) copy-start(bf16[2,1024]{1,0:T(2,128)(2,1)} %taps_ref.1) | copy-start | bytes 12292
  0.7 3.3 %copy-start.2 = (s32[512]{0:T(512)S(1)}, s32[512]{0:T(512)}, u32[]{:S(2)}) copy-start(s32[512]{0:T(512)} %param.10) | copy-start | bytes 6148
